TPU v7x, 32 devices: a whole 2x2x4 slice. The times are simulated.
32 devices in a mesh: groups: 2 (over y), patch: 16 (over z, x, core).
Axes of the slice: x: 2, y: 2, z: 4, core: 2. Of those that a mesh axis runs over, the one named last changes fastest.
Arguments:
- img_q: bfloat16 [256, 1536], P(('groups', 'patch')), parts along dimension 0, may hold values from -40 to 40
- img_kv: bfloat16 [2, 256, 1536], P(None, ('groups', 'patch')), parts along dimension 1, may hold values from -8 to 8
- stale_mant: bfloat16 [2, 256, 1536], P(None, ('groups', 'patch')), parts along dimension 1, may hold values from -2.5 to 2.5
- stale_exp: int32 [2, 256, 12], P(None, ('groups', 'patch')), parts along dimension 1, may hold values from -2 to 1
- txt_q: bfloat16 [512, 1536], P('groups'), parts along dimension 0, may hold values from -48 to 48
- txt_kv: bfloat16 [2, 512, 1536], P(None, 'groups'), parts along dimension 1, may hold values from -8 to 8
- order: int32 [32], P(('groups', 'patch')), parts along dimension 0, may hold values from 0 to 15, as said below
- timestep: int32 [2], P('groups'), parts along dimension 0, may hold values from 0 to 27
- gate_table: float32 [28, 2, 1536], replicated, may hold values from 0.5 to 2
Outputs:
- img_out: bfloat16 [256, 1536], P(('groups', 'patch')), parts along dimension 0
- txt_out: bfloat16 [512, 1536], P('groups'), parts along dimension 0
There are 2 independent parts, one for each index of `groups`. A program takes and returns all parts, laid end to end along the dimension named above; an argument that names none is the same for every part. Nothing has to cross between parts.
Inputs may be any that keep to these rules, and one draw needn't show every extreme that they name: `order`: each patch is held by exactly one device.
All inputs are finite; a program needn't handle non-finite values.
Results may differ from a plain program's by a relative error of at most 0.0063.
Values may be sent and summed in bfloat16 or wider, within the bound.
No kernel may reach another device: no remote copies, remote signals or barrier semaphores. Data moves between devices by JAX's collectives and lax.ppermute only.
A program may use at most 64 MiB of HBM per device.

v0:
```python
import jax
import jax.numpy as jnp
from jax import lax
from jax.sharding import PartitionSpec as P


def rotate_rows(values, position, heads):
    count = values.shape[0]
    head_dim = values.shape[1] // heads
    half = head_dim // 2
    frequency = 10000.0 ** (-jnp.arange(half, dtype=jnp.float32) / half)
    angles = position[:, None] * frequency[None, :]
    cosine = jnp.cos(angles)[:, None, :]
    sine = jnp.sin(angles)[:, None, :]
    split_heads = values.astype(jnp.float32).reshape(count, heads, head_dim)
    first_half = split_heads[..., :half]
    second_half = split_heads[..., half:]
    turned = jnp.concatenate(
        [first_half * cosine - second_half * sine, first_half * sine + second_half * cosine],
        axis=-1,
    )
    return turned.reshape(count, heads * head_dim).astype(jnp.bfloat16)


def partial_state(queries, keys, values, heads):
    query_count = queries.shape[0]
    key_count = keys.shape[0]
    head_dim = queries.shape[1] // heads
    q_heads = queries.reshape(query_count, heads, head_dim)
    k_heads = keys.reshape(key_count, heads, head_dim)
    v_heads = values.reshape(key_count, heads, head_dim)
    scores = jnp.einsum(
        "rhd,shd->rhs", q_heads, k_heads, preferred_element_type=jnp.float32
    ) * head_dim ** (-0.5)
    highest = jnp.max(scores, axis=-1)
    powers = jnp.exp(scores - highest[..., None])
    totals = jnp.sum(powers, axis=-1)
    summed = jnp.einsum(
        "rhs,shd->rhd", powers.astype(jnp.bfloat16), v_heads, preferred_element_type=jnp.float32
    )
    return (highest, totals, summed)


def combine_states(first, second):
    first_max, first_total, first_sum = first
    second_max, second_total, second_sum = second
    highest = jnp.maximum(first_max, second_max)
    first_factor = jnp.exp(first_max - highest)
    second_factor = jnp.exp(second_max - highest)
    totals = first_total * first_factor + second_total * second_factor
    summed = first_sum * first_factor[..., None] + second_sum * second_factor[..., None]
    return (highest, totals, summed)


def on_device(img_q, img_kv, stale_mant, stale_exp, txt_q, txt_kv, order, timestep, gate_table):
    rows = img_q.shape[0]
    width = img_q.shape[1]
    heads = stale_exp.shape[2]
    head_dim = width // heads
    text_rows = txt_q.shape[0]
    place = lax.axis_index("patch")
    position = (order[0] * rows + jnp.arange(rows, dtype=jnp.int32)).astype(jnp.float32)
    q_turned = rotate_rows(img_q, position, heads)
    k_turned = rotate_rows(img_kv[0], position, heads)
    fresh_values = img_kv[1]
    gate = lax.dynamic_index_in_dim(gate_table, timestep[0], 0, keepdims=False)
    start_state = partial_state(
        q_turned,
        jnp.concatenate([txt_kv[0], k_turned], axis=0),
        jnp.concatenate([txt_kv[1], fresh_values], axis=0),
        heads,
    )
    q_heads = q_turned.reshape(rows, heads, head_dim)
    highest, totals, summed = start_state
    mantissa = lax.all_gather(stale_mant, "patch", axis=1, tiled=True)
    exponent = lax.all_gather(stale_exp, "patch", axis=1, tiled=True)
    count = mantissa.shape[1]
    scaling = jnp.exp2(exponent.astype(jnp.float32)).astype(jnp.bfloat16)
    decoded = mantissa.reshape(2, count, heads, head_dim) * scaling[..., None]
    scores = jnp.einsum(
        "rhd,shd->rhs", q_heads, decoded[0], preferred_element_type=jnp.float32
    ) * head_dim ** (-0.5)
    keep_rows = jnp.arange(count, dtype=jnp.int32) // rows != place
    scores = jnp.where(keep_rows[None, None, :], scores, -jnp.inf)
    new_highest = jnp.maximum(highest, jnp.max(scores, axis=-1))
    factor = jnp.exp(highest - new_highest)
    powers = jnp.exp(scores - new_highest[..., None])
    totals = totals * factor + jnp.sum(powers, axis=-1)
    summed = summed * factor[..., None] + jnp.einsum(
        "rhs,shd->rhd", powers.astype(jnp.bfloat16), decoded[1], preferred_element_type=jnp.float32
    )
    image_heads = (summed / totals[..., None]).reshape(rows, width)
    img_out = (gate[0] * image_heads).astype(jnp.bfloat16)
    text_partial = partial_state(txt_q, k_turned, fresh_values, heads)
    global_max = lax.pmax(text_partial[0], "patch")
    factor = jnp.exp(text_partial[0] - global_max)
    scaled_totals = text_partial[1] * factor
    scaled_sums = text_partial[2] * factor[..., None]
    all_totals, all_sums = lax.psum((scaled_totals, scaled_sums), "patch")
    own_state = partial_state(txt_q, txt_kv[0], txt_kv[1], heads)
    final_state = combine_states((global_max, all_totals, all_sums), own_state)
    text_heads = (final_state[2] / final_state[1][..., None]).reshape(text_rows, width)
    txt_out = (gate[1] * text_heads).astype(jnp.bfloat16)
    return (img_out, txt_out)


def solution(mesh):
    in_specs = (
        P(("groups", "patch"), None),
        P(None, ("groups", "patch"), None),
        P(None, ("groups", "patch"), None),
        P(None, ("groups", "patch"), None),
        P("groups", None),
        P(None, "groups", None),
        P(("groups", "patch")),
        P("groups"),
        P(),
    )
    out_specs = (P(("groups", "patch"), None), P("groups", None))
    return jax.shard_map(
        on_device, mesh=mesh, in_specs=in_specs, out_specs=out_specs, check_vma=False
    )
```

profile of v0, /device:TPU:0, one launch (start us, length us, event | category | flops | bytes accessed | tf_op | source)
XLA Modules:
  0.0 214.8 jit_solution(2396789798797518411)
XLA Ops:
  7.2 0.0 all-reduce.2.cloned.1.call-start
  7.9 0.7 bitcast_convert_fusion
  8.6 0.0 copy-start.4
  8.6 0.8 slice_bitcast_fusion.4
  9.5 1.4 copy.73
  10.9 0.0 copy-start
  10.9 0.1 multiply_cosine_fusion
  11.0 0.1 subtract_convert_fusion.1
  11.1 0.3 fusion.59
  11.4 62.9 %pmax.7 = f32[256,12]{0,1:T(8,128)S(1)} all-reduce(f32[256,12]{0,1:T(8,128)S(1)} %get-tuple-element.35), channel_id=1, replica_groups=mesh['groups'=2,'patch'=16] {'patch'}, use_global_device_ids=true, to_apply=%region_5.6 | all-reduce | flops 3072 | bytes 24576 | tf_op jit(solution)/shard_map/pmax | solution.py:95
  74.4 0.0 copy-done.4
  74.4 0.0 copy-start.2
  74.4 1.9 bitcast_multiply_fusion.2
  76.3 0.0 copy-done
  76.3 0.0 all-reduce.2.cloned.1.call-update
  76.3 0.0 copy-done.2
  76.3 1.0 fusion.56
  77.3 0.3 copy.87
  77.6 0.0 copy-start.1
  77.6 0.9 copy-done.1
  78.4 1.2 copy.67
  79.6 0.0 copy-start.6
  79.6 0.0 copy-start.5
  79.6 2.0 bitcast_reduce_fusion
  81.6 0.0 copy-done.6
  81.7 0.0 copy-done.5
  81.7 17.9 %all_gather.7 = s32[2,128,12]{2,0,1:T(2,128)S(1)} all-gather(s32[2,8,12]{2,0,1:T(2,128)S(1)} %copy.70), channel_id=1, replica_groups=mesh['groups'=2,'patch'=16] {'patch'}, dimensions={1}, use_global_device_ids=true | all-gather | bytes 13056 | tf_op jit(solution)/shard_map/all_gather | solution.py:76
  99.6 0.1 copy.71
  99.7 23.0 %all_gather.6 = bf16[2,128,1536]{2,0,1:T(2,128)(2,1)} all-gather(bf16[2,8,1536]{2,0,1:T(2,128)(2,1)S(1)} %copy.68), channel_id=1, replica_groups=mesh['groups'=2,'patch'=16] {'patch'}, dimensions={1}, use_global_device_ids=true | all-gather | bytes 835584 | tf_op jit(solution)/shard_map/all_gather | solution.py:75
  122.7 3.0 %copy.69 = bf16[2,128,1536]{1,2,0:T(8,128)(2,1)} copy(bf16[2,128,1536]{2,0,1:T(2,128)(2,1)} %all_gather.6) | data formatting | bytes 1572864 | tf_op jit(solution)/shard_map/all_gather | solution.py:75
  125.8 2.3 %copy.72 = bf16[2,128,12,128]{3,1,2,0:T(8,128)(2,1)} copy(bf16[2,128,12,128]{1,3,2,0:T(8,128)(2,1)} %bitcast.88) | data formatting | bytes 1572864 | tf_op jit(solution)/shard_map/reshape | solution.py:79
  128.1 1.6 broadcast_multiply_fusion
  129.7 0.0 copy-start.3
  129.7 1.9 fusion.57
  131.6 0.4 fusion.58
  132.0 0.2 fusion.30
  132.2 0.2 fusion.38
  132.4 0.0 copy-done.3
  132.4 0.5 fusion.1
  133.6 2.3 %copy.86 = bf16[1,256,1536]{1,2,0:T(8,128)(2,1)} copy(bf16[1,256,1536]{2,1,0:T(8,128)(2,1)} %get-tuple-element.19) | data formatting | bytes 1572864
  135.9 2.3 %copy.65 = bf16[256,12,128]{2,0,1:T(8,128)(2,1)} copy(bf16[256,12,128]{0,2,1:T(8,128)(2,1)} %bitcast.86) | data formatting | bytes 1572864 | tf_op jit(solution)/shard_map/concatenate | solution.py:70
  138.2 0.8 dynamic-slice_reduce_fusion
  139.0 58.1 %psum.15 = f32[256,12]{0,1:T(8,128)S(1)} all-reduce(f32[256,12]{0,1:T(8,128)S(1)} %get-tuple-element.15), channel_id=1, replica_groups=mesh['groups'=2,'patch'=16] {'patch'}, use_global_device_ids=true, to_apply=%region_9.10 | all-reduce | flops 3072 | bytes 24576 | tf_op jit(solution)/shard_map/psum | solution.py:99
  197.1 1.3 convolution_bitcast_fusion.1
  198.4 2.1 fusion.17
  200.4 0.0 all-reduce.2.cloned.1.call-done
  200.4 4.1 %fusion.7 = f32[256,12,128]{2,0,1:T(8,128)} fusion(f32[256,12,128]{2,0,1:T(8,128)} %all-reduce.2.cloned.1.call-done, bf16[256,12,128]{0,2,1:T(8,128)(2,1)} %bitcast.87, f32[12,256,256]{2,1,0:T(8,128)S(1)} %get-tuple-element.38, f32[256,12]{0,1:T(8,128)S(1)} %get-tuple-element.37, f32[256,12]{0,1:T(8,128)S(1)} %get-tuple-element.12, ...), kind=kOutput, calls=%fused_computation.10 | convolution fusion | flops 205258752 | bytes 7127040 | tf_op jit(solution)/shard_map/rhs,shd->rhd/dot_general | solution.py:38
  204.6 1.9 copy.79
  206.5 0.3 fusion.5
  206.8 1.2 copy.80
  (11 shorter events, 0.2 us)
Async XLA Ops:
  7.2 193.3 %all-reduce.2.cloned.1.call-start = ((), (), s32[]{:S(2)}) async-start(), calls=%async_computation | async-start | bytes 3145728 | tf_op jit(solution)/shard_map/psum | solution.py:99
  8.6 65.7 %copy-start.4 = (bf16[2,8,1536]{2,1,0:T(8,128)(2,1)S(1)}, bf16[2,8,1536]{2,1,0:T(8,128)(2,1)}, u32[]{:S(2)}) copy-start(bf16[2,8,1536]{2,1,0:T(8,128)(2,1)} %param.10) | copy-start | bytes 147460
  10.9 65.4 %copy-start = (bf16[256,1536]{0,1:T(8,128)(2,1)}, bf16[256,1536]{0,1:T(8,128)(2,1)S(1)}, u32[]{:S(2)}) copy-start(bf16[256,1536]{0,1:T(8,128)(2,1)S(1)} %copy.73) | copy-start | bytes 2359300
  74.4 1.9 copy-start.2
  77.6 0.9 copy-start.1
  79.6 2.1 copy-start.6
  79.6 2.1 copy-start.5
  129.7 2.7 %copy-start.3 = (bf16[2,128,12,128]{3,1,2,0:T(8,128)(2,1)}, bf16[2,128,12,128]{3,1,2,0:T(8,128)(2,1)S(1)}, u32[]{:S(2)}) copy-start(bf16[2,128,12,128]{3,1,2,0:T(8,128)(2,1)S(1)} %broadcast_multiply_fusion) | copy-start | bytes 2359300
Sparse Core Ops, SparseCore 0:
  76.4 93.6 all-reduce.1
where the time goes:
time: 216 us; the launch traced here: 215 us
  blocking collectives  162 us (75%)
  local copies, waits for them, and re-layouts  18.6 us (9%)
  between operations  15.6 us (7%)
  matrix products  14 us (6%)
  other arithmetic  4.67 us (2%)
    pmax x1, blocking collectives, on_device(): global_max = lax.pmax(text_partial[0], 'patch')  62.9 us
    psum x1, blocking collectives, on_device(): all_totals, all_sums = lax.psum((scaled_totals, scaled_sums), 'patch')  58.1 us
    all_gather x1, blocking collectives, on_device(): mantissa = lax.all_gather(stale_mant, 'patch', axis=1, tiled=True)  23 us
    all_gather x1, blocking collectives, on_device(): exponent = lax.all_gather(stale_exp, 'patch', axis=1, tiled=True)  17.9 us
    dot_general x3, matrix products, partial_state(): jnp.einsum('rhs,shd->rhd', powers.astype(jnp.bfloat16), v_heads, preferre...  8.08 us
    unnamed x20, local copies, waits for them, and re-layouts  6.06 us
  transfers between devices with their start and end apart: 1, of which 0 were waited for; matrix products, arithmetic and copies ran while one was open for 11% of the time, Pallas kernels for 0%

commit v1 on v0

v1 whole, which is shorter than its diff:
```python
import functools
import math

import jax
import jax.numpy as jnp
from jax import lax
from jax.experimental import pallas as pl
from jax.experimental.pallas import tpu as pltpu
from jax.sharding import PartitionSpec as P

VMEM = pl.BlockSpec(memory_space=pltpu.VMEM)
SMEM = pl.BlockSpec(memory_space=pltpu.SMEM)
NT = (((1,), (1,)), ((), ()))
LOG2E = 1.4426950408889634


def turn_tables(first, rows, head_dim):
    half = head_dim // 2
    lane = lax.broadcasted_iota(jnp.int32, (rows, head_dim), 1)
    row = lax.broadcasted_iota(jnp.int32, (rows, head_dim), 0)
    low = lane < half
    index = jnp.where(low, lane, lane - half).astype(jnp.float32)
    frequency = jnp.exp(index * (-math.log(10000.0) / half))
    angles = (first + row).astype(jnp.float32) * frequency
    sine = jnp.sin(angles)
    return jnp.cos(angles), jnp.where(low, -sine, sine)


def turn(x, cosine, sine):
    return x * cosine + pltpu.roll(x, x.shape[1] // 2, axis=1) * sine


def pack_kernel(order_ref, kv_ref, mant_ref, exp_ref, block_ref):
    rows, width = kv_ref.shape[1:]
    heads = exp_ref.shape[2]
    head_dim = width // heads
    cosine, sine = turn_tables(order_ref[0] * rows, rows, head_dim)
    for which in range(2):
        power = jnp.exp2(exp_ref[which].astype(jnp.float32))
        power = power.astype(jnp.bfloat16).astype(jnp.float32)
        for head in range(heads):
            span = slice(head * head_dim, (head + 1) * head_dim)
            fresh = kv_ref[which, :, span].astype(jnp.float32)
            if which == 0:
                fresh = turn(fresh, cosine, sine)
            stale = mant_ref[which, :, span].astype(jnp.float32) * power[:, head : head + 1]
            both = jnp.concatenate([fresh, stale], axis=0).astype(jnp.bfloat16)
            start = which * width + head * head_dim
            block_ref[:, start : start + head_dim] = both


def attend(queries, keys, values, scale):
    scores = lax.dot_general(queries, keys, NT, preferred_element_type=jnp.float32)
    highest = jnp.max(scores, axis=-1, keepdims=True)
    powers = jnp.exp2((scores - highest) * scale)
    totals = jnp.sum(powers, axis=-1, keepdims=True)
    summed = jnp.dot(powers.astype(jnp.bfloat16), values, preferred_element_type=jnp.float32)
    return summed / totals


def attend_kernel(heads, rows, order_ref, time_ref, gate_ref, q_ref, txt_q_ref, txt_kv_ref, *refs):
    blocks, (img_out_ref, txt_out_ref) = refs[:-2], refs[-2:]
    width = q_ref.shape[1]
    head_dim = width // heads
    scale = head_dim ** (-0.5) * LOG2E
    cosine, sine = turn_tables(order_ref[0] * rows, rows, head_dim)
    for head in range(heads):
        span = slice(head * head_dim, (head + 1) * head_dim)
        parts = []
        for which in range(2):
            start = which * width + head * head_dim
            fresh, stale = [], []
            for number, block in enumerate(blocks):
                for place in range(block.shape[0]):
                    both = block[place, :, start : start + head_dim].astype(jnp.float32)
                    own = number == 0 and place == 0
                    fresh.append(both[:rows])
                    stale.append(both[:rows] if own else both[rows:])
            parts.append([jnp.concatenate(p, axis=0).astype(jnp.bfloat16) for p in (fresh, stale)])
        (new_keys, old_keys), (new_values, old_values) = parts
        txt_keys, txt_values = txt_kv_ref[0, :, span], txt_kv_ref[1, :, span]
        text = attend(
            txt_q_ref[:, span],
            jnp.concatenate([txt_keys, new_keys], axis=0),
            jnp.concatenate([txt_values, new_values], axis=0),
            scale,
        )
        txt_out_ref[:, span] = (text * gate_ref[0, 1:2, span]).astype(jnp.bfloat16)
        queries = turn(q_ref[:, span].astype(jnp.float32), cosine, sine).astype(jnp.bfloat16)
        image = attend(
            queries,
            jnp.concatenate([txt_keys, old_keys], axis=0),
            jnp.concatenate([txt_values, old_values], axis=0),
            scale,
        )
        img_out_ref[:, span] = (image * gate_ref[0, 0:1, span]).astype(jnp.bfloat16)


def swap(x, even, odd=None):
    odd = even if odd is None else odd
    count = lax.axis_size("patch")
    pairs = [(i, i ^ (odd if i % 2 else even)) for i in range(count)]
    return lax.ppermute(x, "patch", pairs)


def gather_blocks(block):
    count = lax.axis_size("patch")
    block = block[None]
    if count == 16:
        hops = ((2, 8), (8, 4), (4, 2))
        one, two, three = (swap(block, *hop) for hop in hops)
        one_two = swap(one, *hops[1])
        one_three = swap(one, *hops[2])
        two_three = swap(two, *hops[2])
        all_three = swap(one_two, *hops[2])
        blocks = [block, one, two, three, one_two, one_three, two_three, all_three]
        return blocks + [swap(b, 1) for b in blocks]
    if count & (count - 1) == 0:
        bit = count // 2
        while bit:
            block = jnp.concatenate([block, swap(block, bit)], axis=0)
            bit //= 2
        return [block]
    blocks = [block]
    ring = [(i, (i + 1) % count) for i in range(count)]
    for _ in range(count - 1):
        blocks.append(lax.ppermute(blocks[-1], "patch", ring))
    return blocks


def on_device(img_q, img_kv, stale_mant, stale_exp, txt_q, txt_kv, order, timestep, gate_table):
    rows, width = img_q.shape
    heads = stale_exp.shape[2]
    block = pl.pallas_call(
        pack_kernel,
        out_shape=jax.ShapeDtypeStruct((2 * rows, 2 * width), jnp.bfloat16),
        in_specs=[SMEM, VMEM, VMEM, VMEM],
        out_specs=VMEM,
        name="pack",
    )(order, img_kv, stale_mant, stale_exp)
    blocks = gather_blocks(block)
    gate = lax.dynamic_index_in_dim(gate_table, timestep[0], 0, keepdims=True)
    return pl.pallas_call(
        functools.partial(attend_kernel, heads, rows),
        out_shape=(
            jax.ShapeDtypeStruct(img_q.shape, jnp.bfloat16),
            jax.ShapeDtypeStruct(txt_q.shape, jnp.bfloat16),
        ),
        in_specs=[SMEM, SMEM] + [VMEM] * (4 + len(blocks)),
        out_specs=(VMEM, VMEM),
        compiler_params=pltpu.CompilerParams(vmem_limit_bytes=40 << 20),
        name="attend",
    )(order, timestep, gate, img_q, txt_q, txt_kv, *blocks)


def solution(mesh):
    in_specs = (
        P(("groups", "patch"), None),
        P(None, ("groups", "patch"), None),
        P(None, ("groups", "patch"), None),
        P(None, ("groups", "patch"), None),
        P("groups", None),
        P(None, "groups", None),
        P(("groups", "patch")),
        P("groups"),
        P(),
    )
    out_specs = (P(("groups", "patch"), None), P("groups", None))
    return jax.shard_map(
        on_device, mesh=mesh, in_specs=in_specs, out_specs=out_specs, check_vma=False
    )
```

time: 216 us -> 34.5 us (0.16)
  blocking collectives: 162 us -> 0 us
  local copies, waits for them, and re-layouts: 18.6 us -> 4.18 us
  matrix products: 14 us -> 0 us
  between operations: 15.6 us -> 2.05 us
  starting transfers between devices: 0.04 us -> 11.8 us
  Pallas kernels: 0 us -> 9.04 us
  waiting for transfers between devices: 0.02 us -> 7.08 us
  other arithmetic: 4.67 us -> 0 us
    pmax x1 -> x0, blocking collectives: 62.9 us -> none  [on_device(): global_max = lax.pmax(text_partial[0], 'patch')]
    psum x1 -> x0, blocking collectives: 58.1 us -> none  [on_device(): all_totals, all_sums = lax.psum((scaled_totals, scaled_sums), 'patch')]
    all_gather x2 -> x0, blocking collectives: 40.9 us -> none  [the longest x1 23 us: on_device(): mantissa = lax.all_gather(stale_mant, 'patch', axis=1, tiled=True)]
    dot_general x8 -> x0, matrix products: 14 us -> none  [the longest x3 8.08 us: partial_state(): jnp.einsum('rhs,shd->rhd', powers.astype(jnp.bfloat16), v_heads, preferre...]
    ppermute x0 -> x15, starting transfers between devices: none -> 11.8 us  [swap(): return lax.ppermute(x, 'patch', pairs)]
    pallas_call x0 -> x2, Pallas kernels: none -> 9.04 us  [the longest x1 7.48 us: on_device(): pl.pallas_call(functools.partial(attend_kernel, heads, rows), out_shape=(...]
    ppermute x0 -> x15, waiting for transfers between devices: none -> 7.08 us  [swap(): return lax.ppermute(x, 'patch', pairs)]
    concatenate x2 -> x0, local copies, waits for them, and re-layouts: 3.44 us -> none  [the longest x1 2.29 us: on_device(): jnp.concatenate([txt_kv[1], fresh_values], axis=0)]
  transfers between devices with their start and end apart: 1 -> 15, of which waited for: 0 -> 6; matrix products, arithmetic and copies ran while one was open for 11% -> 0% of each run, Pallas kernels for 0% -> 0%
where the time goes in v1:
time: 34.5 us; the launch traced here: 34.2 us
  starting transfers between devices  11.8 us (34%)
  Pallas kernels  9.04 us (26%)
  waiting for transfers between devices  7.08 us (21%)
  local copies, waits for them, and re-layouts  4.18 us (12%)
  between operations  2.05 us (6%)
    ppermute x15, starting transfers between devices, swap(): return lax.ppermute(x, 'patch', pairs)  11.8 us
    pallas_call x1, Pallas kernels, on_device(): pl.pallas_call(functools.partial(attend_kernel, heads, rows), out_shape=(...  7.48 us
    ppermute x15, waiting for transfers between devices, swap(): return lax.ppermute(x, 'patch', pairs)  7.08 us
    unnamed x10, local copies, waits for them, and re-layouts  4.18 us
    pallas_call x1, Pallas kernels, on_device(): pl.pallas_call(pack_kernel, out_shape=jax.ShapeDtypeStruct((2 * rows, 2 *...  1.57 us
  transfers between devices with their start and end apart: 15, of which 6 were waited for; matrix products, arithmetic and copies ran while one was open for 0% of the time, Pallas kernels for 0%

profile of v1, /device:TPU:0, one launch (start us, length us, event | category | flops | bytes accessed | tf_op | source)
XLA Modules:
  0.0 34.2 jit_solution(567466721578118097)
XLA Ops:
  0.6 0.0 copy-start
  1.3 1.6 %pack.1 = bf16[16,3072]{1,0:T(8,128)(2,1)} custom-call(s32[1]{0:T(128)S(6)} %copy.11.order_ref, bf16[2,8,1536]{2,1,0:T(8,128)(2,1)} %kv_ref.1, bf16[2,8,1536]{2,1,0:T(8,128)(2,1)} %mant_ref.1, s32[2,8,12]{2,1,0:T(8,128)} %exp_ref.1), custom_call_target="tpu_custom_call" | custom-call | tf_op jit(solution)/shard_map/pack/pallas_call | solution.py:134
  2.9 2.9 %collective-permute-start = (bf16[1,16,3072]{2,1,0:T(8,128)(2,1)}, bf16[1,16,3072]{2,1,0:T(8,128)(2,1)S(1)}, u32[]{:S(2)}, u32[]{:S(2)}) collective-permute-start(bf16[1,16,3072]{2,1,0:T(8,128)(2,1)} %bitcast.5), channel_id=1, source_target_pairs={{0,2},{1,9},{2,0},{3,11},{4,6},{5,13},{6,4},{7,15},{8,10},{9,1},{1... | collective-permute-start | bytes 294920 | tf_op jit(solution)/shard_map/ppermute | solution.py:103
  5.8 1.6 %collective-permute-start.2 = (bf16[1,16,3072]{2,1,0:T(8,128)(2,1)}, bf16[1,16,3072]{2,1,0:T(8,128)(2,1)S(1)}, u32[]{:S(2)}, u32[]{:S(2)}) collective-permute-start(bf16[1,16,3072]{2,1,0:T(8,128)(2,1)} %bitcast.6), channel_id=1, source_target_pairs={{0,4},{1,3},{2,6},{3,1},{4,0},{5,7},{6,2},{7,5},{8,12},{9,11},{10,... | collective-permute-start | bytes 294920 | tf_op jit(solution)/shard_map/ppermute | solution.py:103
  7.4 2.6 %collective-permute-start.1 = (bf16[1,16,3072]{2,1,0:T(8,128)(2,1)}, bf16[1,16,3072]{2,1,0:T(8,128)(2,1)S(1)}, u32[]{:S(2)}, u32[]{:S(2)}) collective-permute-start(bf16[1,16,3072]{2,1,0:T(8,128)(2,1)} %bitcast.7), channel_id=1, source_target_pairs={{0,8},{1,5},{2,10},{3,7},{4,12},{5,1},{6,14},{7,3},{8,0},{9,13},{1... | collective-permute-start | bytes 294920 | tf_op jit(solution)/shard_map/ppermute | solution.py:103
  10.0 0.0 collective-permute-start.7
  10.0 0.0 collective-permute-done.refs_1_
  10.0 1.8 %collective-permute-start.3 = (bf16[1,16,3072]{2,1,0:T(8,128)(2,1)S(1)}, bf16[1,16,3072]{2,1,0:T(8,128)(2,1)S(1)}, u32[]{:S(2)}, u32[]{:S(2)}) collective-permute-start(bf16[1,16,3072]{2,1,0:T(8,128)(2,1)S(1)} %collective-permute-done.refs_1_), channel_id=1, source_target_pairs={{0,8},{1,5},{2,10},{3,7},{4,12},{5,1},{6,14},{7,3},{8,0},{9,13},{1... | collective-permute-start | bytes 294920 | tf_op jit(solution)/shard_map/ppermute | solution.py:103
  11.8 0.0 collective-permute-done.2.refs_3_
  11.8 0.0 collective-permute-start.10
  11.8 2.5 %collective-permute-done.1.refs_2_ = bf16[1,16,3072]{2,1,0:T(8,128)(2,1)S(1)} collective-permute-done((bf16[1,16,3072]{2,1,0:T(8,128)(2,1)}, bf16[1,16,3072]{2,1,0:T(8,128)(2,1)S(1)}, u32[]{:S(2)}, u32[]{:S(2)}) %collective-permute-start.1) | collective-permute-done | bytes 98336 | tf_op jit(solution)/shard_map/ppermute | solution.py:103
  14.3 0.0 collective-permute-start.9
  14.3 0.1 collective-permute-start.5
  14.4 0.0 collective-permute-done.7.refs_8_
  14.4 1.9 %collective-permute-start.4 = (bf16[1,16,3072]{2,1,0:T(8,128)(2,1)S(1)}, bf16[1,16,3072]{2,1,0:T(8,128)(2,1)S(1)}, u32[]{:S(2)}, u32[]{:S(2)}) collective-permute-start(bf16[1,16,3072]{2,1,0:T(8,128)(2,1)S(1)} %collective-permute-done.refs_1_), channel_id=1, source_target_pairs={{0,4},{1,3},{2,6},{3,1},{4,0},{5,7},{6,2},{7,5},{8,12},{9,11},{10,... | collective-permute-start | bytes 294920 | tf_op jit(solution)/shard_map/ppermute | solution.py:103
  16.3 0.2 collective-permute-done.3.refs_4_
  16.6 0.3 %collective-permute-start.6 = (bf16[1,16,3072]{2,1,0:T(8,128)(2,1)S(1)}, bf16[1,16,3072]{2,1,0:T(8,128)(2,1)S(1)}, u32[]{:S(2)}, u32[]{:S(2)}) collective-permute-start(bf16[1,16,3072]{2,1,0:T(8,128)(2,1)S(1)} %collective-permute-done.3.refs_4_), channel_id=1, source_target_pairs={{0,4},{1,3},{2,6},{3,1},{4,0},{5,7},{6,2},{7,5},{8,12},{9,11},{10,... | collective-permute-start | bytes 294920 | tf_op jit(solution)/shard_map/ppermute | solution.py:103
  17.6 0.0 collective-permute-done.10.refs_11_
  17.6 0.1 collective-permute-start.8
  17.7 0.0 collective-permute-done.9.refs_10_
  17.7 0.5 %collective-permute-start.11 = (bf16[1,16,3072]{2,1,0:T(8,128)(2,1)S(1)}, bf16[1,16,3072]{2,1,0:T(8,128)(2,1)S(1)}, u32[]{:S(2)}, u32[]{:S(2)}) collective-permute-start(bf16[1,16,3072]{2,1,0:T(8,128)(2,1)S(1)} %collective-permute-done.3.refs_4_), channel_id=1, source_target_pairs={{0,1},{1,0},{2,3},{3,2},{4,5},{5,4},{6,7},{7,6},{8,9},{9,8},{10,11... | collective-permute-start | bytes 294920 | tf_op jit(solution)/shard_map/ppermute | solution.py:103
  18.2 0.7 %collective-permute-done.5.refs_6_ = bf16[1,16,3072]{2,1,0:T(8,128)(2,1)S(1)} collective-permute-done((bf16[1,16,3072]{2,1,0:T(8,128)(2,1)S(1)}, bf16[1,16,3072]{2,1,0:T(8,128)(2,1)S(1)}, u32[]{:S(2)}, u32[]{:S(2)}) %collective-permute-start.5) | collective-permute-done | bytes 98336 | tf_op jit(solution)/shard_map/ppermute | solution.py:103
  18.9 0.0 collective-permute-start.13
  18.9 1.0 %collective-permute-done.4.refs_5_ = bf16[1,16,3072]{2,1,0:T(8,128)(2,1)S(1)} collective-permute-done((bf16[1,16,3072]{2,1,0:T(8,128)(2,1)S(1)}, bf16[1,16,3072]{2,1,0:T(8,128)(2,1)S(1)}, u32[]{:S(2)}, u32[]{:S(2)}) %collective-permute-start.4) | collective-permute-done | bytes 98336 | tf_op jit(solution)/shard_map/ppermute | solution.py:103
  20.0 0.0 collective-permute-start.12
  20.0 1.2 %collective-permute-done.6.refs_7_ = bf16[1,16,3072]{2,1,0:T(8,128)(2,1)S(1)} collective-permute-done((bf16[1,16,3072]{2,1,0:T(8,128)(2,1)S(1)}, bf16[1,16,3072]{2,1,0:T(8,128)(2,1)S(1)}, u32[]{:S(2)}, u32[]{:S(2)}) %collective-permute-start.6) | collective-permute-done | bytes 98336 | tf_op jit(solution)/shard_map/ppermute | solution.py:103
  21.2 0.0 collective-permute-start.14
  21.2 0.0 copy-done
  21.2 0.0 collective-permute-done.8.refs_9_
  21.2 0.0 collective-permute-done.13.refs_14_
  21.2 0.0 collective-permute-done.12.refs_13_
  21.3 0.0 collective-permute-done.11.refs_12_
  21.3 1.2 %collective-permute-done.14.refs_15_ = bf16[1,16,3072]{2,1,0:T(8,128)(2,1)S(1)} collective-permute-done((bf16[1,16,3072]{2,1,0:T(8,128)(2,1)S(1)}, bf16[1,16,3072]{2,1,0:T(8,128)(2,1)S(1)}, u32[]{:S(2)}, u32[]{:S(2)}) %collective-permute-start.14) | collective-permute-done | bytes 98336 | tf_op jit(solution)/shard_map/ppermute | solution.py:103
  22.5 0.0 copy-start.1
  22.5 1.4 %copy-done.1 = bf16[2,256,1536]{2,1,0:T(8,128)(2,1)S(1)} copy-done((bf16[2,256,1536]{2,1,0:T(8,128)(2,1)S(1)}, bf16[2,256,1536]{2,1,0:T(8,128)(2,1)}, u32[]{:S(2)}) %copy-start.1) | copy-done | bytes 1572888
  23.9 0.0 copy-start.2
  23.9 1.1 %copy-done.2 = bf16[256,1536]{1,0:T(8,128)(2,1)S(1)} copy-done((bf16[256,1536]{1,0:T(8,128)(2,1)S(1)}, bf16[256,1536]{1,0:T(8,128)(2,1)}, u32[]{:S(2)}) %copy-start.2) | copy-done | bytes 786456
  25.1 0.0 copy-start.3
  25.1 0.9 %copy-done.3 = bf16[16,3072]{1,0:T(8,128)(2,1)S(1)} copy-done((bf16[16,3072]{1,0:T(8,128)(2,1)S(1)}, bf16[16,3072]{1,0:T(8,128)(2,1)}, u32[]{:S(2)}) %copy-start.3) | copy-done | bytes 98328
  25.9 0.0 copy-start.4
  25.9 0.7 %copy-done.4 = bf16[8,1536]{1,0:T(8,128)(2,1)S(1)} copy-done((bf16[8,1536]{1,0:T(8,128)(2,1)S(1)}, bf16[8,1536]{1,0:T(8,128)(2,1)}, u32[]{:S(2)}) %copy-start.4) | copy-done | bytes 24600
  26.7 7.5 %attend.1 = (bf16[8,1536]{1,0:T(8,128)(2,1)}, bf16[256,1536]{1,0:T(8,128)(2,1)}) custom-call(s32[1]{0:T(128)S(6)} %copy.11.order_ref, s32[1]{0:T(128)} %copy.12.time_ref, f32[1,2,1536]{2,1,0:T(2,128)S(1)} %constant_dynamic-slice_fusion.gate_ref, bf16[8,1536]{1,0:T(8,128)(2,1)S(1)} %copy-done.4, bf16[256,1536]{1,0:T(8,128)(2,1)S(1)} %copy-done.2, ...), custom_call_target="tpu_custom_call" | custom-call | tf_op jit(solution)/shard_map/attend/pallas_call | solution.py:143
  (1 shorter events, 0.0 us)
Async XLA Ops:
  0.6 20.6 %copy-start = (f32[28,2,1536]{2,1,0:T(2,128)S(1)}, f32[28,2,1536]{2,1,0:T(2,128)}, u32[]{:S(2)}) copy-start(f32[28,2,1536]{2,1,0:T(2,128)} %param.17) | copy-start | bytes 1032196
  2.9 7.1 %collective-permute-start = (bf16[1,16,3072]{2,1,0:T(8,128)(2,1)}, bf16[1,16,3072]{2,1,0:T(8,128)(2,1)S(1)}, u32[]{:S(2)}, u32[]{:S(2)}) collective-permute-start(bf16[1,16,3072]{2,1,0:T(8,128)(2,1)} %bitcast.5), channel_id=1, source_target_pairs={{0,2},{1,9},{2,0},{3,11},{4,6},{5,13},{6,4},{7,15},{8,10},{9,1},{1... | collective-permute-start | bytes 294920 | tf_op jit(solution)/shard_map/ppermute | solution.py:103
  5.8 5.9 %collective-permute-start.2 = (bf16[1,16,3072]{2,1,0:T(8,128)(2,1)}, bf16[1,16,3072]{2,1,0:T(8,128)(2,1)S(1)}, u32[]{:S(2)}, u32[]{:S(2)}) collective-permute-start(bf16[1,16,3072]{2,1,0:T(8,128)(2,1)} %bitcast.6), channel_id=1, source_target_pairs={{0,4},{1,3},{2,6},{3,1},{4,0},{5,7},{6,2},{7,5},{8,12},{9,11},{10,... | collective-permute-start | bytes 294920 | tf_op jit(solution)/shard_map/ppermute | solution.py:103
  7.4 6.9 %collective-permute-start.1 = (bf16[1,16,3072]{2,1,0:T(8,128)(2,1)}, bf16[1,16,3072]{2,1,0:T(8,128)(2,1)S(1)}, u32[]{:S(2)}, u32[]{:S(2)}) collective-permute-start(bf16[1,16,3072]{2,1,0:T(8,128)(2,1)} %bitcast.7), channel_id=1, source_target_pairs={{0,8},{1,5},{2,10},{3,7},{4,12},{5,1},{6,14},{7,3},{8,0},{9,13},{1... | collective-permute-start | bytes 294920 | tf_op jit(solution)/shard_map/ppermute | solution.py:103
  10.0 4.4 %collective-permute-start.7 = (bf16[1,16,3072]{2,1,0:T(8,128)(2,1)}, bf16[1,16,3072]{2,1,0:T(8,128)(2,1)S(1)}, u32[]{:S(2)}, u32[]{:S(2)}) collective-permute-start(bf16[1,16,3072]{2,1,0:T(8,128)(2,1)} %bitcast.8), channel_id=1, source_target_pairs={{0,1},{1,0},{2,3},{3,2},{4,5},{5,4},{6,7},{7,6},{8,9},{9,8},{10,11... | collective-permute-start | bytes 294920 | tf_op jit(solution)/shard_map/ppermute | solution.py:103
  10.0 6.6 %collective-permute-start.3 = (bf16[1,16,3072]{2,1,0:T(8,128)(2,1)S(1)}, bf16[1,16,3072]{2,1,0:T(8,128)(2,1)S(1)}, u32[]{:S(2)}, u32[]{:S(2)}) collective-permute-start(bf16[1,16,3072]{2,1,0:T(8,128)(2,1)S(1)} %collective-permute-done.refs_1_), channel_id=1, source_target_pairs={{0,8},{1,5},{2,10},{3,7},{4,12},{5,1},{6,14},{7,3},{8,0},{9,13},{1... | collective-permute-start | bytes 294920 | tf_op jit(solution)/shard_map/ppermute | solution.py:103
  11.8 5.8 %collective-permute-start.10 = (bf16[1,16,3072]{2,1,0:T(8,128)(2,1)S(1)}, bf16[1,16,3072]{2,1,0:T(8,128)(2,1)S(1)}, u32[]{:S(2)}, u32[]{:S(2)}) collective-permute-start(bf16[1,16,3072]{2,1,0:T(8,128)(2,1)S(1)} %collective-permute-done.2.refs_3_), channel_id=1, source_target_pairs={{0,1},{1,0},{2,3},{3,2},{4,5},{5,4},{6,7},{7,6},{8,9},{9,8},{10,11... | collective-permute-start | bytes 294920 | tf_op jit(solution)/shard_map/ppermute | solution.py:103
  14.3 3.4 %collective-permute-start.9 = (bf16[1,16,3072]{2,1,0:T(8,128)(2,1)S(1)}, bf16[1,16,3072]{2,1,0:T(8,128)(2,1)S(1)}, u32[]{:S(2)}, u32[]{:S(2)}) collective-permute-start(bf16[1,16,3072]{2,1,0:T(8,128)(2,1)S(1)} %collective-permute-done.1.refs_2_), channel_id=1, source_target_pairs={{0,1},{1,0},{2,3},{3,2},{4,5},{5,4},{6,7},{7,6},{8,9},{9,8},{10,11... | collective-permute-start | bytes 294920 | tf_op jit(solution)/shard_map/ppermute | solution.py:103
  14.3 4.6 %collective-permute-start.5 = (bf16[1,16,3072]{2,1,0:T(8,128)(2,1)S(1)}, bf16[1,16,3072]{2,1,0:T(8,128)(2,1)S(1)}, u32[]{:S(2)}, u32[]{:S(2)}) collective-permute-start(bf16[1,16,3072]{2,1,0:T(8,128)(2,1)S(1)} %collective-permute-done.1.refs_2_), channel_id=1, source_target_pairs={{0,4},{1,3},{2,6},{3,1},{4,0},{5,7},{6,2},{7,5},{8,12},{9,11},{10,... | collective-permute-start | bytes 294920 | tf_op jit(solution)/shard_map/ppermute | solution.py:103
  14.4 5.6 %collective-permute-start.4 = (bf16[1,16,3072]{2,1,0:T(8,128)(2,1)S(1)}, bf16[1,16,3072]{2,1,0:T(8,128)(2,1)S(1)}, u32[]{:S(2)}, u32[]{:S(2)}) collective-permute-start(bf16[1,16,3072]{2,1,0:T(8,128)(2,1)S(1)} %collective-permute-done.refs_1_), channel_id=1, source_target_pairs={{0,4},{1,3},{2,6},{3,1},{4,0},{5,7},{6,2},{7,5},{8,12},{9,11},{10,... | collective-permute-start | bytes 294920 | tf_op jit(solution)/shard_map/ppermute | solution.py:103
  16.6 4.6 %collective-permute-start.6 = (bf16[1,16,3072]{2,1,0:T(8,128)(2,1)S(1)}, bf16[1,16,3072]{2,1,0:T(8,128)(2,1)S(1)}, u32[]{:S(2)}, u32[]{:S(2)}) collective-permute-start(bf16[1,16,3072]{2,1,0:T(8,128)(2,1)S(1)} %collective-permute-done.3.refs_4_), channel_id=1, source_target_pairs={{0,4},{1,3},{2,6},{3,1},{4,0},{5,7},{6,2},{7,5},{8,12},{9,11},{10,... | collective-permute-start | bytes 294920 | tf_op jit(solution)/shard_map/ppermute | solution.py:103
  17.6 3.6 %collective-permute-start.8 = (bf16[1,16,3072]{2,1,0:T(8,128)(2,1)S(1)}, bf16[1,16,3072]{2,1,0:T(8,128)(2,1)S(1)}, u32[]{:S(2)}, u32[]{:S(2)}) collective-permute-start(bf16[1,16,3072]{2,1,0:T(8,128)(2,1)S(1)} %collective-permute-done.refs_1_), channel_id=1, source_target_pairs={{0,1},{1,0},{2,3},{3,2},{4,5},{5,4},{6,7},{7,6},{8,9},{9,8},{10,11... | collective-permute-start | bytes 294920 | tf_op jit(solution)/shard_map/ppermute | solution.py:103
  17.7 3.6 %collective-permute-start.11 = (bf16[1,16,3072]{2,1,0:T(8,128)(2,1)S(1)}, bf16[1,16,3072]{2,1,0:T(8,128)(2,1)S(1)}, u32[]{:S(2)}, u32[]{:S(2)}) collective-permute-start(bf16[1,16,3072]{2,1,0:T(8,128)(2,1)S(1)} %collective-permute-done.3.refs_4_), channel_id=1, source_target_pairs={{0,1},{1,0},{2,3},{3,2},{4,5},{5,4},{6,7},{7,6},{8,9},{9,8},{10,11... | collective-permute-start | bytes 294920 | tf_op jit(solution)/shard_map/ppermute | solution.py:103
  18.9 2.3 %collective-permute-start.13 = (bf16[1,16,3072]{2,1,0:T(8,128)(2,1)S(1)}, bf16[1,16,3072]{2,1,0:T(8,128)(2,1)S(1)}, u32[]{:S(2)}, u32[]{:S(2)}) collective-permute-start(bf16[1,16,3072]{2,1,0:T(8,128)(2,1)S(1)} %collective-permute-done.5.refs_6_), channel_id=1, source_target_pairs={{0,1},{1,0},{2,3},{3,2},{4,5},{5,4},{6,7},{7,6},{8,9},{9,8},{10,11... | collective-permute-start | bytes 294920 | tf_op jit(solution)/shard_map/ppermute | solution.py:103
  20.0 1.3 %collective-permute-start.12 = (bf16[1,16,3072]{2,1,0:T(8,128)(2,1)S(1)}, bf16[1,16,3072]{2,1,0:T(8,128)(2,1)S(1)}, u32[]{:S(2)}, u32[]{:S(2)}) collective-permute-start(bf16[1,16,3072]{2,1,0:T(8,128)(2,1)S(1)} %collective-permute-done.4.refs_5_), channel_id=1, source_target_pairs={{0,1},{1,0},{2,3},{3,2},{4,5},{5,4},{6,7},{7,6},{8,9},{9,8},{10,11... | collective-permute-start | bytes 294920 | tf_op jit(solution)/shard_map/ppermute | solution.py:103
  21.2 1.3 %collective-permute-start.14 = (bf16[1,16,3072]{2,1,0:T(8,128)(2,1)S(1)}, bf16[1,16,3072]{2,1,0:T(8,128)(2,1)S(1)}, u32[]{:S(2)}, u32[]{:S(2)}) collective-permute-start(bf16[1,16,3072]{2,1,0:T(8,128)(2,1)S(1)} %collective-permute-done.6.refs_7_), channel_id=1, source_target_pairs={{0,1},{1,0},{2,3},{3,2},{4,5},{5,4},{6,7},{7,6},{8,9},{9,8},{10,11... | collective-permute-start | bytes 294920 | tf_op jit(solution)/shard_map/ppermute | solution.py:103
  22.5 1.4 %copy-start.1 = (bf16[2,256,1536]{2,1,0:T(8,128)(2,1)S(1)}, bf16[2,256,1536]{2,1,0:T(8,128)(2,1)}, u32[]{:S(2)}) copy-start(bf16[2,256,1536]{2,1,0:T(8,128)(2,1)} %txt_kv_ref.1) | copy-start | bytes 4718596
  23.9 1.1 %copy-start.2 = (bf16[256,1536]{1,0:T(8,128)(2,1)S(1)}, bf16[256,1536]{1,0:T(8,128)(2,1)}, u32[]{:S(2)}) copy-start(bf16[256,1536]{1,0:T(8,128)(2,1)} %txt_q_ref.1) | copy-start | bytes 2359300
  25.1 0.9 %copy-start.3 = (bf16[16,3072]{1,0:T(8,128)(2,1)S(1)}, bf16[16,3072]{1,0:T(8,128)(2,1)}, u32[]{:S(2)}) copy-start(bf16[16,3072]{1,0:T(8,128)(2,1)} %pack.1) | copy-start | bytes 294916
  25.9 0.7 %copy-start.4 = (bf16[8,1536]{1,0:T(8,128)(2,1)S(1)}, bf16[8,1536]{1,0:T(8,128)(2,1)}, u32[]{:S(2)}) copy-start(bf16[8,1536]{1,0:T(8,128)(2,1)} %q_ref.1) | copy-start | bytes 73732

commit v2 on v1

v2 whole, which is shorter than its diff:
```python
import functools
import math

import jax
import jax.numpy as jnp
from jax import lax
from jax.experimental import pallas as pl
from jax.experimental.pallas import tpu as pltpu
from jax.sharding import PartitionSpec as P

VMEM = pl.BlockSpec(memory_space=pltpu.VMEM)
HBM = pl.BlockSpec(memory_space=pltpu.HBM)
SMEM = pl.BlockSpec(memory_space=pltpu.SMEM)
NT = (((1,), (1,)), ((), ()))
LOG2E = 1.4426950408889634
HIDDEN = -1e30
HOPS = ((2, 8), (8, 4), (4, 2))


def turn_tables(first, rows, head_dim):
    half = head_dim // 2
    lane = lax.broadcasted_iota(jnp.int32, (rows, head_dim), 1)
    row = lax.broadcasted_iota(jnp.int32, (rows, head_dim), 0)
    low = lane < half
    index = jnp.where(low, lane, lane - half).astype(jnp.float32)
    frequency = jnp.exp(index * (-math.log(10000.0) / half))
    angles = (first + row).astype(jnp.float32) * frequency
    sine = jnp.sin(angles)
    return jnp.cos(angles), jnp.where(low, -sine, sine)


def turn(x, cosine, sine):
    return x * cosine + pltpu.roll(x, x.shape[1] // 2, axis=1) * sine


def pack_kernel(order_ref, kv_hbm, mant_hbm, exp_hbm, block_ref, kv, mant, exp, sems):
    copies = [
        pltpu.make_async_copy(source, target, sems.at[i])
        for i, (source, target) in enumerate(((exp_hbm, exp), (kv_hbm, kv), (mant_hbm, mant)))
    ]
    for copy in copies:
        copy.start()
    rows, width = kv.shape[1:]
    heads = exp.shape[2]
    head_dim = width // heads
    cosine, sine = turn_tables(order_ref[...] * rows, rows, head_dim)
    for copy in copies:
        copy.wait()
    for which in range(2):
        power = jnp.exp2(exp[which].astype(jnp.float32))
        power = power.astype(jnp.bfloat16).astype(jnp.float32)
        for head in range(heads):
            span = slice(head * head_dim, (head + 1) * head_dim)
            fresh = kv[which, :, span].astype(jnp.float32)
            if which == 0:
                fresh = turn(fresh, cosine, sine)
            stale = mant[which, :, span].astype(jnp.float32) * power[:, head : head + 1]
            both = jnp.concatenate([fresh, stale], axis=0).astype(jnp.bfloat16)
            start = which * width + head * head_dim
            block_ref[:, start : start + head_dim] = both


def join_copies(blocks, joined_ref, sems):
    copies = []
    place = 0
    for i, block in enumerate(blocks):
        span = pl.ds(place, block.shape[0])
        copies.append(pltpu.make_async_copy(block, joined_ref.at[span], sems.at[i]))
        place += block.shape[0]
    return copies


def with_ones(values):
    return jnp.concatenate([values, jnp.ones_like(values)], axis=1)


def text_kernel(heads, count, *refs):
    order_ref, q_hbm, txt_q_hbm, txt_kv_hbm = refs[:4]
    blocks = refs[4 : 4 + count]
    joined_ref, txt_q, turned_ref, mean_ref, level_ref = refs[4 + count : 9 + count]
    q, txt_kv, powers_ref, sems, join_sems = refs[9 + count :]
    q_copy = pltpu.make_async_copy(q_hbm, q, sems.at[0])
    txt_q_copy = pltpu.make_async_copy(txt_q_hbm, txt_q, sems.at[1])
    keys_copy = pltpu.make_async_copy(txt_kv_hbm.at[0], txt_kv.at[0], sems.at[2])
    values_copy = pltpu.make_async_copy(txt_kv_hbm.at[1], txt_kv.at[1], sems.at[3])
    joins = join_copies(blocks, joined_ref, join_sems)
    for copy in [q_copy, txt_q_copy, keys_copy, values_copy] + joins:
        copy.start()
    rows, width = q.shape
    head_dim = width // heads
    scale = head_dim ** (-0.5) * LOG2E
    cosine, sine = turn_tables(order_ref[...] * rows, rows, head_dim)
    q_copy.wait()
    for head in range(heads):
        span = slice(head * head_dim, (head + 1) * head_dim)
        turned = turn(q[:, span].astype(jnp.float32), cosine, sine)
        turned_ref[:, span] = turned.astype(jnp.bfloat16)
    txt_q_copy.wait()
    keys_copy.wait()
    for head in range(heads):
        span = slice(head * head_dim, (head + 1) * head_dim)
        queries = jnp.concatenate([txt_q[:, span], turned_ref[:, span]], axis=0)
        scores = lax.dot_general(queries, txt_kv[0, :, span], NT, preferred_element_type=jnp.float32)
        scores = scores * scale
        highest = jnp.max(scores, axis=-1, keepdims=True)
        powers_ref[head] = jnp.exp2(scores - highest).astype(jnp.bfloat16)
        level_ref[:, span] = jnp.broadcast_to(highest, (highest.shape[0], head_dim))
    values_copy.wait()
    for head in range(heads):
        span = slice(head * head_dim, (head + 1) * head_dim)
        summed = jnp.dot(
            powers_ref[head], with_ones(txt_kv[1, :, span]), preferred_element_type=jnp.float32
        )
        mean_ref[:, span] = summed[:, :head_dim] / summed[:, head_dim:]
        level_ref[:, span] = level_ref[:, span] + jnp.log2(summed[:, head_dim:])
    for copy in joins:
        copy.wait()


def image_kernel(heads, time_ref, gate_hbm, txt_q_ref, turned_ref, mean_ref, level_ref, *refs):
    blocks = refs[:-5]
    img_out_ref, txt_out_ref, gate, held, gate_sem = refs[-5:]
    gate_copy = pltpu.make_async_copy(gate_hbm.at[time_ref[0]], gate, gate_sem)
    gate_copy.start()
    rows, width = img_out_ref.shape
    head_dim = width // heads
    text_rows = txt_q_ref.shape[0]
    scale = head_dim ** (-0.5) * LOG2E
    columns = 2 * rows * sum(block.shape[0] for block in blocks)
    column = lax.broadcasted_iota(jnp.int32, (rows, columns), 1)
    fresh = lax.rem(column, 2 * rows) < rows
    no_stale = jnp.where(fresh, 0.0, HIDDEN)
    no_fresh = jnp.where(fresh, HIDDEN, 0.0)
    image_mask = jnp.where(column < 2 * rows, no_stale, no_fresh)
    text_mask = jnp.broadcast_to(no_stale[:1], (text_rows, columns))
    mask = jnp.concatenate([text_mask, image_mask], axis=0)
    def store(head, result):
        span = slice(head * head_dim, (head + 1) * head_dim)
        txt_out_ref[:, span] = (result[:text_rows] * gate[1:2, span]).astype(jnp.bfloat16)
        img_out_ref[:, span] = (result[text_rows:] * gate[0:1, span]).astype(jnp.bfloat16)

    waiting = held.shape[0]
    for head in range(heads):
        span = slice(head * head_dim, (head + 1) * head_dim)
        keys, values = (
            jnp.concatenate(
                [
                    block[i, :, start : start + head_dim]
                    for block in blocks
                    for i in range(block.shape[0])
                ],
                axis=0,
            )
            for start in (head * head_dim, width + head * head_dim)
        )
        queries = jnp.concatenate([txt_q_ref[:, span], turned_ref[:, span]], axis=0)
        scores = lax.dot_general(queries, keys, NT, preferred_element_type=jnp.float32)
        scores = scores * scale + mask
        level = level_ref[:, span]
        highest = jnp.maximum(level, jnp.max(scores, axis=-1, keepdims=True))
        weight = jnp.exp2(level - highest)
        powers = jnp.exp2(scores - jnp.concatenate([highest] * (columns // head_dim), axis=1))
        summed = jnp.dot(
            powers.astype(jnp.bfloat16), with_ones(values), preferred_element_type=jnp.float32
        )
        result = (mean_ref[:, span] * weight + summed[:, :head_dim]) / (weight + summed[:, head_dim:])
        if head < waiting:
            held[head] = result
            if head == waiting - 1:
                gate_copy.wait()
                for early in range(waiting):
                    store(early, held[early])
        else:
            store(head, result)


def swap(x, even, odd=None):
    odd = even if odd is None else odd
    count = lax.axis_size("patch")
    pairs = [(i, i ^ (odd if i % 2 else even)) for i in range(count)]
    return lax.ppermute(x, "patch", pairs)


def gather_columns(block):
    count = lax.axis_size("patch")
    block = block[None]
    if count == 16:
        hops = HOPS
        one = swap(block, *hops[0])
        three = swap(block, *hops[2])
        one_two = swap(one, *hops[1])
        two = swap(block, *hops[1])
        one_three = swap(one, *hops[2])
        two_three = swap(two, *hops[2])
        all_three = swap(one_two, *hops[2])
        return [block, one, two, three, one_two], [one_three, two_three, all_three]
    if count & (count - 1) == 0:
        bit = count // 2
        while bit:
            block = jnp.concatenate([block, swap(block, bit)], axis=0)
            bit //= 2
        return [block], []
    blocks = [block]
    ring = [(i, (i + 1) % count) for i in range(count)]
    for _ in range(count - 1):
        blocks.append(lax.ppermute(blocks[-1], "patch", ring))
    return blocks, []


def on_device(img_q, img_kv, stale_mant, stale_exp, txt_q, txt_kv, order, timestep, gate_table):
    rows, width = img_q.shape
    heads = stale_exp.shape[2]
    text_rows = txt_q.shape[0]
    all_rows = text_rows + rows
    bf16, f32 = jnp.bfloat16, jnp.float32
    img_q, img_kv, stale_mant, stale_exp, gate_table, txt_q, txt_kv = (
        pltpu.with_memory_space_constraint(x, pltpu.HBM)
        for x in (img_q, img_kv, stale_mant, stale_exp, gate_table, txt_q, txt_kv)
    )
    order = order.reshape(1, 1)
    block = pl.pallas_call(
        pack_kernel,
        out_shape=pltpu.VMEM((2 * rows, 2 * width), bf16),
        in_specs=[VMEM] + [HBM] * 3,
        out_specs=VMEM,
        scratch_shapes=[
            pltpu.VMEM(img_kv.shape, img_kv.dtype),
            pltpu.VMEM(stale_mant.shape, stale_mant.dtype),
            pltpu.VMEM(stale_exp.shape, stale_exp.dtype),
            pltpu.SemaphoreType.DMA((3,)),
        ],
        name="pack",
    )(order, img_kv, stale_mant, stale_exp)
    early, late = gather_columns(block)
    joined = sum(x.shape[0] for x in early)
    first, *states = pl.pallas_call(
        functools.partial(text_kernel, heads, len(early)),
        out_shape=(
            pltpu.VMEM((joined,) + block.shape, bf16),
            pltpu.VMEM(txt_q.shape, bf16),
            pltpu.VMEM((rows, width), bf16),
            pltpu.VMEM((all_rows, width), f32),
            pltpu.VMEM((all_rows, width), f32),
        ),
        in_specs=[VMEM] + [HBM] * 3 + [VMEM] * len(early),
        out_specs=[VMEM] * 5,
        scratch_shapes=[
            pltpu.VMEM(img_q.shape, img_q.dtype),
            pltpu.VMEM(txt_kv.shape, txt_kv.dtype),
            pltpu.VMEM((heads, all_rows, text_rows), bf16),
            pltpu.SemaphoreType.DMA((4,)),
            pltpu.SemaphoreType.DMA((len(early),)),
        ],
        compiler_params=pltpu.CompilerParams(vmem_limit_bytes=16 << 20),
        name="text",
    )(order, img_q, txt_q, txt_kv, *early)
    blocks = [first] + late
    if lax.axis_size("patch") == 16:
        blocks = list(lax.optimization_barrier(tuple(blocks)))
        blocks += [swap(x, 1) for x in blocks]
    return pl.pallas_call(
        functools.partial(image_kernel, heads),
        out_shape=(
            jax.ShapeDtypeStruct(img_q.shape, bf16),
            jax.ShapeDtypeStruct(txt_q.shape, bf16),
        ),
        in_specs=[SMEM, HBM] + [VMEM] * (len(states) + len(blocks)),
        out_specs=(VMEM, VMEM),
        scratch_shapes=[
            pltpu.VMEM(gate_table.shape[1:], f32),
            pltpu.VMEM((6, all_rows, width // heads), f32),
            pltpu.SemaphoreType.DMA,
        ],
        compiler_params=pltpu.CompilerParams(vmem_limit_bytes=32 << 20),
        name="image",
    )(timestep, gate_table, *states, *blocks)


def solution(mesh):
    in_specs = (
        P(("groups", "patch"), None),
        P(None, ("groups", "patch"), None),
        P(None, ("groups", "patch"), None),
        P(None, ("groups", "patch"), None),
        P("groups", None),
        P(None, "groups", None),
        P(("groups", "patch")),
        P("groups"),
        P(),
    )
    out_specs = (P(("groups", "patch"), None), P("groups", None))
    return jax.shard_map(
        on_device, mesh=mesh, in_specs=in_specs, out_specs=out_specs, check_vma=False
    )
```

time: 34.5 us -> 24.6 us (0.71)
  waiting for transfers between devices: 7.08 us -> 0.86 us
  local copies, waits for them, and re-layouts: 4.18 us -> 0 us
  starting transfers between devices: 11.8 us -> 14.8 us
  Pallas kernels: 9.04 us -> 6.64 us
    ppermute x15 -> x11, waiting for transfers between devices: 7.08 us -> 0.86 us  [swap(): return lax.ppermute(x, 'patch', pairs)]
    unnamed x10 -> x0, local copies, waits for them, and re-layouts: 4.18 us -> none
    ppermute x15 -> x11, starting transfers between devices: 11.8 us -> 14.8 us  [swap(): return lax.ppermute(x, 'patch', pairs)]
    pallas_call x2 -> x3, Pallas kernels: 9.04 us -> 6.64 us  [the longest x1 2.98 us: on_device(): pl.pallas_call(functools.partial(text_kernel, heads, len(early)), out_sha...]
  transfers between devices with their start and end apart: 15 -> 11, of which waited for: 6 -> 4; matrix products, arithmetic and copies ran while one was open for 0% -> 0% of each run, Pallas kernels for 0% -> 12%
where the time goes in v2:
time: 24.6 us; the launch traced here: 24.3 us
  starting transfers between devices  14.8 us (60%)
  Pallas kernels  6.64 us (27%)
  between operations  1.97 us (8%)
  waiting for transfers between devices  0.86 us (3%)
    ppermute x11, starting transfers between devices, swap(): return lax.ppermute(x, 'patch', pairs)  14.8 us
    pallas_call x1, Pallas kernels, on_device(): pl.pallas_call(functools.partial(text_kernel, heads, len(early)), out_sha...  2.98 us
    pallas_call x1, Pallas kernels, on_device(): pl.pallas_call(functools.partial(image_kernel, heads), out_shape=(jax.Sha...  2.69 us
    pallas_call x1, Pallas kernels, on_device(): pl.pallas_call(pack_kernel, out_shape=pltpu.VMEM((2 * rows, 2 * width), b...  0.97 us
    ppermute x11, waiting for transfers between devices, swap(): return lax.ppermute(x, 'patch', pairs)  0.86 us
  transfers between devices with their start and end apart: 11, of which 4 were waited for; matrix products, arithmetic and copies ran while one was open for 0% of the time, Pallas kernels for 12%

profile of v2, /device:TPU:0, one launch (start us, length us, event | category | flops | bytes accessed | tf_op | source)
XLA Modules:
  0.0 24.3 jit_solution(17898889710808136542)
XLA Ops:
  1.3 1.0 %pack.1 = bf16[16,3072]{1,0:T(8,128)(2,1)S(1)} custom-call(s32[1,1]{1,0:T(1,128)} %bitcast.2.order_ref, bf16[2,8,1536]{2,1,0:T(8,128)(2,1)} %kv_hbm.1, bf16[2,8,1536]{2,1,0:T(8,128)(2,1)} %mant_hbm.1, s32[2,8,12]{2,1,0:T(8,128)} %exp_hbm.1), custom_call_target="tpu_custom_call" | custom-call | tf_op jit(solution)/shard_map/pack/pallas_call | solution.py:221
  2.3 3.0 %collective-permute-start = (bf16[1,16,3072]{2,1,0:T(8,128)(2,1)S(1)}, bf16[1,16,3072]{2,1,0:T(8,128)(2,1)S(1)}, u32[]{:S(2)}, u32[]{:S(2)}) collective-permute-start(bf16[1,16,3072]{2,1,0:T(8,128)(2,1)S(1)} %bitcast.4), channel_id=1, source_target_pairs={{0,2},{1,9},{2,0},{3,11},{4,6},{5,13},{6,4},{7,15},{8,10},{9,1},{1... | collective-permute-start | bytes 294920 | tf_op jit(solution)/shard_map/ppermute | solution.py:181
  5.3 2.6 %collective-permute-start.1 = (bf16[1,16,3072]{2,1,0:T(8,128)(2,1)S(1)}, bf16[1,16,3072]{2,1,0:T(8,128)(2,1)S(1)}, u32[]{:S(2)}, u32[]{:S(2)}) collective-permute-start(bf16[1,16,3072]{2,1,0:T(8,128)(2,1)S(1)} %bitcast.5), channel_id=1, source_target_pairs={{0,8},{1,5},{2,10},{3,7},{4,12},{5,1},{6,14},{7,3},{8,0},{9,13},{1... | collective-permute-start | bytes 294920 | tf_op jit(solution)/shard_map/ppermute | solution.py:181
  7.8 0.0 collective-permute-done.refs_5_
  7.9 3.1 %collective-permute-start.3 = (bf16[1,16,3072]{2,1,0:T(8,128)(2,1)S(1)}, bf16[1,16,3072]{2,1,0:T(8,128)(2,1)S(1)}, u32[]{:S(2)}, u32[]{:S(2)}) collective-permute-start(bf16[1,16,3072]{2,1,0:T(8,128)(2,1)S(1)} %collective-permute-done.refs_5_), channel_id=1, source_target_pairs={{0,8},{1,5},{2,10},{3,7},{4,12},{5,1},{6,14},{7,3},{8,0},{9,13},{1... | collective-permute-start | bytes 294920 | tf_op jit(solution)/shard_map/ppermute | solution.py:181
  11.0 1.6 %collective-permute-start.2 = (bf16[1,16,3072]{2,1,0:T(8,128)(2,1)S(1)}, bf16[1,16,3072]{2,1,0:T(8,128)(2,1)S(1)}, u32[]{:S(2)}, u32[]{:S(2)}) collective-permute-start(bf16[1,16,3072]{2,1,0:T(8,128)(2,1)S(1)} %bitcast.6), channel_id=1, source_target_pairs={{0,4},{1,3},{2,6},{3,1},{4,0},{5,7},{6,2},{7,5},{8,12},{9,11},{10,... | collective-permute-start | bytes 294920 | tf_op jit(solution)/shard_map/ppermute | solution.py:181
  12.5 0.4 %collective-permute-start.4 = (bf16[1,16,3072]{2,1,0:T(8,128)(2,1)S(1)}, bf16[1,16,3072]{2,1,0:T(8,128)(2,1)S(1)}, u32[]{:S(2)}, u32[]{:S(2)}) collective-permute-start(bf16[1,16,3072]{2,1,0:T(8,128)(2,1)S(1)} %collective-permute-done.refs_5_), channel_id=1, source_target_pairs={{0,4},{1,3},{2,6},{3,1},{4,0},{5,7},{6,2},{7,5},{8,12},{9,11},{10,... | collective-permute-start | bytes 294920 | tf_op jit(solution)/shard_map/ppermute | solution.py:181
  13.0 0.0 collective-permute-done.1.refs_6_
  13.0 1.6 %collective-permute-start.5 = (bf16[1,16,3072]{2,1,0:T(8,128)(2,1)S(1)}, bf16[1,16,3072]{2,1,0:T(8,128)(2,1)S(1)}, u32[]{:S(2)}, u32[]{:S(2)}) collective-permute-start(bf16[1,16,3072]{2,1,0:T(8,128)(2,1)S(1)} %collective-permute-done.1.refs_6_), channel_id=1, source_target_pairs={{0,4},{1,3},{2,6},{3,1},{4,0},{5,7},{6,2},{7,5},{8,12},{9,11},{10,... | collective-permute-start | bytes 294920 | tf_op jit(solution)/shard_map/ppermute | solution.py:181
  14.6 0.0 collective-permute-done.3.refs_8_
  14.6 1.4 %collective-permute-start.6 = (bf16[1,16,3072]{2,1,0:T(8,128)(2,1)S(1)}, bf16[1,16,3072]{2,1,0:T(8,128)(2,1)S(1)}, u32[]{:S(2)}, u32[]{:S(2)}) collective-permute-start(bf16[1,16,3072]{2,1,0:T(8,128)(2,1)S(1)} %collective-permute-done.3.refs_8_), channel_id=1, source_target_pairs={{0,4},{1,3},{2,6},{3,1},{4,0},{5,7},{6,2},{7,5},{8,12},{9,11},{10,... | collective-permute-start | bytes 294920 | tf_op jit(solution)/shard_map/ppermute | solution.py:181
  16.0 0.0 collective-permute-done.2.refs_7_
  16.0 3.0 %text.1 = (bf16[5,16,3072]{2,1,0:T(8,128)(2,1)S(1)}, bf16[256,1536]{1,0:T(8,128)(2,1)S(1)}, bf16[8,1536]{1,0:T(8,128)(2,1)S(1)}, f32[264,1536]{1,0:T(8,128)S(1)}, f32[264,1536]{1,0:T(8,128)S(1)}) custom-call(s32[1,1]{1,0:T(1,128)} %bitcast.3.refs_0_, bf16[8,1536]{1,0:T(8,128)(2,1)} %refs_1_.1, bf16[256,1536]{1,0:T(8,128)(2,1)} %refs_2_.1, ...), custom_call_target="tpu_custom_call" | custom-call | tf_op jit(solution)/shard_map/text/pallas_call | solution.py:236
  19.0 0.0 collective-permute-done.5.refs_2_
  19.0 0.0 collective-permute-done.4.refs_1_
  19.0 0.2 collective-permute-done.6.refs_3_
  19.3 0.0 collective-permute-start.7
  19.3 0.5 %collective-permute-start.8 = (bf16[1,16,3072]{2,1,0:T(8,128)(2,1)S(1)}, bf16[1,16,3072]{2,1,0:T(8,128)(2,1)S(1)}, u32[]{:S(2)}, u32[]{:S(2)}) collective-permute-start(bf16[1,16,3072]{2,1,0:T(8,128)(2,1)S(1)} %collective-permute-done.4.refs_1_), channel_id=1, source_target_pairs={{0,1},{1,0},{2,3},{3,2},{4,5},{5,4},{6,7},{7,6},{8,9},{9,8},{10,11... | collective-permute-start | bytes 294920 | tf_op jit(solution)/shard_map/ppermute | solution.py:181
  19.8 0.0 collective-permute-start.9
  19.8 0.5 %collective-permute-start.10 = (bf16[1,16,3072]{2,1,0:T(8,128)(2,1)S(1)}, bf16[1,16,3072]{2,1,0:T(8,128)(2,1)S(1)}, u32[]{:S(2)}, u32[]{:S(2)}) collective-permute-start(bf16[1,16,3072]{2,1,0:T(8,128)(2,1)S(1)} %collective-permute-done.6.refs_3_), channel_id=1, source_target_pairs={{0,1},{1,0},{2,3},{3,2},{4,5},{5,4},{6,7},{7,6},{8,9},{9,8},{10,11... | collective-permute-start | bytes 294920 | tf_op jit(solution)/shard_map/ppermute | solution.py:181
  20.9 0.3 %collective-permute-done.8.refs_5_ = bf16[1,16,3072]{2,1,0:T(8,128)(2,1)S(1)} collective-permute-done((bf16[1,16,3072]{2,1,0:T(8,128)(2,1)S(1)}, bf16[1,16,3072]{2,1,0:T(8,128)(2,1)S(1)}, u32[]{:S(2)}, u32[]{:S(2)}) %collective-permute-start.8) | collective-permute-done | bytes 98336 | tf_op jit(solution)/shard_map/ppermute | solution.py:181
  21.3 0.1 collective-permute-done.9.refs_6_
  21.4 0.1 collective-permute-done.10.refs_7_
  21.6 0.0 collective-permute-done.7.refs_4_
  21.6 2.7 %image.1 = (bf16[8,1536]{1,0:T(8,128)(2,1)}, bf16[256,1536]{1,0:T(8,128)(2,1)}) custom-call(s32[1]{0:T(128)S(6)} %copy.12.time_ref, f32[28,2,1536]{2,1,0:T(2,128)} %gate_hbm.1, bf16[256,1536]{1,0:T(8,128)(2,1)S(1)} %get-tuple-element.11.txt_q_ref, bf16[8,1536]{1,0:T(8,128)(2,1)S(1)} %get-tuple-element.12.turned_ref, ...), custom_call_target="tpu_custom_call" | custom-call | tf_op jit(solution)/shard_map/image/pallas_call | solution.py:261
Async XLA Ops:
  2.3 5.6 %collective-permute-start = (bf16[1,16,3072]{2,1,0:T(8,128)(2,1)S(1)}, bf16[1,16,3072]{2,1,0:T(8,128)(2,1)S(1)}, u32[]{:S(2)}, u32[]{:S(2)}) collective-permute-start(bf16[1,16,3072]{2,1,0:T(8,128)(2,1)S(1)} %bitcast.4), channel_id=1, source_target_pairs={{0,2},{1,9},{2,0},{3,11},{4,6},{5,13},{6,4},{7,15},{8,10},{9,1},{1... | collective-permute-start | bytes 294920 | tf_op jit(solution)/shard_map/ppermute | solution.py:181
  5.3 7.7 %collective-permute-start.1 = (bf16[1,16,3072]{2,1,0:T(8,128)(2,1)S(1)}, bf16[1,16,3072]{2,1,0:T(8,128)(2,1)S(1)}, u32[]{:S(2)}, u32[]{:S(2)}) collective-permute-start(bf16[1,16,3072]{2,1,0:T(8,128)(2,1)S(1)} %bitcast.5), channel_id=1, source_target_pairs={{0,8},{1,5},{2,10},{3,7},{4,12},{5,1},{6,14},{7,3},{8,0},{9,13},{1... | collective-permute-start | bytes 294920 | tf_op jit(solution)/shard_map/ppermute | solution.py:181
  7.9 6.7 %collective-permute-start.3 = (bf16[1,16,3072]{2,1,0:T(8,128)(2,1)S(1)}, bf16[1,16,3072]{2,1,0:T(8,128)(2,1)S(1)}, u32[]{:S(2)}, u32[]{:S(2)}) collective-permute-start(bf16[1,16,3072]{2,1,0:T(8,128)(2,1)S(1)} %collective-permute-done.refs_5_), channel_id=1, source_target_pairs={{0,8},{1,5},{2,10},{3,7},{4,12},{5,1},{6,14},{7,3},{8,0},{9,13},{1... | collective-permute-start | bytes 294920 | tf_op jit(solution)/shard_map/ppermute | solution.py:181
  11.0 5.1 %collective-permute-start.2 = (bf16[1,16,3072]{2,1,0:T(8,128)(2,1)S(1)}, bf16[1,16,3072]{2,1,0:T(8,128)(2,1)S(1)}, u32[]{:S(2)}, u32[]{:S(2)}) collective-permute-start(bf16[1,16,3072]{2,1,0:T(8,128)(2,1)S(1)} %bitcast.6), channel_id=1, source_target_pairs={{0,4},{1,3},{2,6},{3,1},{4,0},{5,7},{6,2},{7,5},{8,12},{9,11},{10,... | collective-permute-start | bytes 294920 | tf_op jit(solution)/shard_map/ppermute | solution.py:181
  12.5 6.5 %collective-permute-start.4 = (bf16[1,16,3072]{2,1,0:T(8,128)(2,1)S(1)}, bf16[1,16,3072]{2,1,0:T(8,128)(2,1)S(1)}, u32[]{:S(2)}, u32[]{:S(2)}) collective-permute-start(bf16[1,16,3072]{2,1,0:T(8,128)(2,1)S(1)} %collective-permute-done.refs_5_), channel_id=1, source_target_pairs={{0,4},{1,3},{2,6},{3,1},{4,0},{5,7},{6,2},{7,5},{8,12},{9,11},{10,... | collective-permute-start | bytes 294920 | tf_op jit(solution)/shard_map/ppermute | solution.py:181
  13.0 6.0 %collective-permute-start.5 = (bf16[1,16,3072]{2,1,0:T(8,128)(2,1)S(1)}, bf16[1,16,3072]{2,1,0:T(8,128)(2,1)S(1)}, u32[]{:S(2)}, u32[]{:S(2)}) collective-permute-start(bf16[1,16,3072]{2,1,0:T(8,128)(2,1)S(1)} %collective-permute-done.1.refs_6_), channel_id=1, source_target_pairs={{0,4},{1,3},{2,6},{3,1},{4,0},{5,7},{6,2},{7,5},{8,12},{9,11},{10,... | collective-permute-start | bytes 294920 | tf_op jit(solution)/shard_map/ppermute | solution.py:181
  14.6 4.7 %collective-permute-start.6 = (bf16[1,16,3072]{2,1,0:T(8,128)(2,1)S(1)}, bf16[1,16,3072]{2,1,0:T(8,128)(2,1)S(1)}, u32[]{:S(2)}, u32[]{:S(2)}) collective-permute-start(bf16[1,16,3072]{2,1,0:T(8,128)(2,1)S(1)} %collective-permute-done.3.refs_8_), channel_id=1, source_target_pairs={{0,4},{1,3},{2,6},{3,1},{4,0},{5,7},{6,2},{7,5},{8,12},{9,11},{10,... | collective-permute-start | bytes 294920 | tf_op jit(solution)/shard_map/ppermute | solution.py:181
  19.3 2.3 %collective-permute-start.7 = (bf16[5,16,3072]{2,1,0:T(8,128)(2,1)S(1)}, bf16[5,16,3072]{2,1,0:T(8,128)(2,1)S(1)}, u32[]{:S(2)}, u32[]{:S(2)}) collective-permute-start(bf16[5,16,3072]{2,1,0:T(8,128)(2,1)S(1)} %get-tuple-element.16.refs_0_), channel_id=1, source_target_pairs={{0,1},{1,0},{2,3},{3,2},{4,5},{5,4},{6,7},{7,6},{8,9},{9,8},{10,11... | collective-permute-start | bytes 1474568 | tf_op jit(solution)/shard_map/ppermute | solution.py:181
  19.3 2.0 %collective-permute-start.8 = (bf16[1,16,3072]{2,1,0:T(8,128)(2,1)S(1)}, bf16[1,16,3072]{2,1,0:T(8,128)(2,1)S(1)}, u32[]{:S(2)}, u32[]{:S(2)}) collective-permute-start(bf16[1,16,3072]{2,1,0:T(8,128)(2,1)S(1)} %collective-permute-done.4.refs_1_), channel_id=1, source_target_pairs={{0,1},{1,0},{2,3},{3,2},{4,5},{5,4},{6,7},{7,6},{8,9},{9,8},{10,11... | collective-permute-start | bytes 294920 | tf_op jit(solution)/shard_map/ppermute | solution.py:181
  19.8 1.6 %collective-permute-start.9 = (bf16[1,16,3072]{2,1,0:T(8,128)(2,1)S(1)}, bf16[1,16,3072]{2,1,0:T(8,128)(2,1)S(1)}, u32[]{:S(2)}, u32[]{:S(2)}) collective-permute-start(bf16[1,16,3072]{2,1,0:T(8,128)(2,1)S(1)} %collective-permute-done.5.refs_2_), channel_id=1, source_target_pairs={{0,1},{1,0},{2,3},{3,2},{4,5},{5,4},{6,7},{7,6},{8,9},{9,8},{10,11... | collective-permute-start | bytes 294920 | tf_op jit(solution)/shard_map/ppermute | solution.py:181
  19.8 1.8 %collective-permute-start.10 = (bf16[1,16,3072]{2,1,0:T(8,128)(2,1)S(1)}, bf16[1,16,3072]{2,1,0:T(8,128)(2,1)S(1)}, u32[]{:S(2)}, u32[]{:S(2)}) collective-permute-start(bf16[1,16,3072]{2,1,0:T(8,128)(2,1)S(1)} %collective-permute-done.6.refs_3_), channel_id=1, source_target_pairs={{0,1},{1,0},{2,3},{3,2},{4,5},{5,4},{6,7},{7,6},{8,9},{9,8},{10,11... | collective-permute-start | bytes 294920 | tf_op jit(solution)/shard_map/ppermute | solution.py:181

commit v3 on v2

--- a/solution.py
+++ b/solution.py
@@ -14,7 +14,7 @@
 NT = (((1,), (1,)), ((), ()))
 LOG2E = 1.4426950408889634
 HIDDEN = -1e30
-HOPS = ((2, 8), (8, 4), (4, 2))
+HOPS = ((2, 12), (8, 4), (4, 2))
 
 
 def turn_tables(first, rows, head_dim):
@@ -60,31 +60,34 @@
             block_ref[:, start : start + head_dim] = both
 
 
-def join_copies(blocks, joined_ref, sems):
-    copies = []
-    place = 0
-    for i, block in enumerate(blocks):
-        span = pl.ds(place, block.shape[0])
-        copies.append(pltpu.make_async_copy(block, joined_ref.at[span], sems.at[i]))
-        place += block.shape[0]
-    return copies
+def join_kernel(*refs):
+    for i, block in enumerate(refs[:-1]):
+        refs[-1][i] = block[0]
+
+
+def join(*blocks):
+    return pl.pallas_call(
+        join_kernel,
+        out_shape=pltpu.VMEM((len(blocks),) + blocks[0].shape[1:], blocks[0].dtype),
+        in_specs=[VMEM] * len(blocks),
+        out_specs=VMEM,
+        compiler_params=pltpu.CompilerParams(vmem_limit_bytes=2 << 20),
+        name="join",
+    )(*blocks)
 
 
 def with_ones(values):
     return jnp.concatenate([values, jnp.ones_like(values)], axis=1)
 
 
-def text_kernel(heads, count, *refs):
-    order_ref, q_hbm, txt_q_hbm, txt_kv_hbm = refs[:4]
-    blocks = refs[4 : 4 + count]
-    joined_ref, txt_q, turned_ref, mean_ref, level_ref = refs[4 + count : 9 + count]
-    q, txt_kv, powers_ref, sems, join_sems = refs[9 + count :]
+def text_first_kernel(heads, share, order_ref, q_hbm, txt_q_hbm, txt_kv_hbm, gate_hbm, *refs):
+    gate_ref, txt_q, txt_kv, turned_ref, mean_ref, level_ref, q, powers_ref, sems = refs
     q_copy = pltpu.make_async_copy(q_hbm, q, sems.at[0])
     txt_q_copy = pltpu.make_async_copy(txt_q_hbm, txt_q, sems.at[1])
     keys_copy = pltpu.make_async_copy(txt_kv_hbm.at[0], txt_kv.at[0], sems.at[2])
     values_copy = pltpu.make_async_copy(txt_kv_hbm.at[1], txt_kv.at[1], sems.at[3])
-    joins = join_copies(blocks, joined_ref, join_sems)
-    for copy in [q_copy, txt_q_copy, keys_copy, values_copy] + joins:
+    gate_copy = pltpu.make_async_copy(gate_hbm, gate_ref, sems.at[4])
+    for copy in (q_copy, txt_q_copy, keys_copy, values_copy, gate_copy):
         copy.start()
     rows, width = q.shape
     head_dim = width // heads
@@ -97,7 +100,7 @@
         turned_ref[:, span] = turned.astype(jnp.bfloat16)
     txt_q_copy.wait()
     keys_copy.wait()
-    for head in range(heads):
+    for head in range(share):
         span = slice(head * head_dim, (head + 1) * head_dim)
         queries = jnp.concatenate([txt_q[:, span], turned_ref[:, span]], axis=0)
         scores = lax.dot_general(queries, txt_kv[0, :, span], NT, preferred_element_type=jnp.float32)
@@ -106,22 +109,35 @@
         powers_ref[head] = jnp.exp2(scores - highest).astype(jnp.bfloat16)
         level_ref[:, span] = jnp.broadcast_to(highest, (highest.shape[0], head_dim))
     values_copy.wait()
-    for head in range(heads):
+    for head in range(share):
         span = slice(head * head_dim, (head + 1) * head_dim)
         summed = jnp.dot(
             powers_ref[head], with_ones(txt_kv[1, :, span]), preferred_element_type=jnp.float32
         )
         mean_ref[:, span] = summed[:, :head_dim] / summed[:, head_dim:]
         level_ref[:, span] = level_ref[:, span] + jnp.log2(summed[:, head_dim:])
-    for copy in joins:
-        copy.wait()
-
-
-def image_kernel(heads, time_ref, gate_hbm, txt_q_ref, turned_ref, mean_ref, level_ref, *refs):
-    blocks = refs[:-5]
-    img_out_ref, txt_out_ref, gate, held, gate_sem = refs[-5:]
-    gate_copy = pltpu.make_async_copy(gate_hbm.at[time_ref[0]], gate, gate_sem)
-    gate_copy.start()
+    gate_copy.wait()
+
+
+def text_second_kernel(heads, first, txt_q, txt_kv, turned_ref, mean_ref, level_ref):
+    head_dim = txt_q.shape[1] // heads
+    scale = head_dim ** (-0.5) * LOG2E
+    for head in range(first, heads):
+        span = slice(head * head_dim, (head + 1) * head_dim)
+        here = slice((head - first) * head_dim, (head - first + 1) * head_dim)
+        queries = jnp.concatenate([txt_q[:, span], turned_ref[:, span]], axis=0)
+        scores = lax.dot_general(queries, txt_kv[0, :, span], NT, preferred_element_type=jnp.float32)
+        scores = scores * scale
+        highest = jnp.max(scores, axis=-1, keepdims=True)
+        powers = jnp.exp2(scores - highest).astype(jnp.bfloat16)
+        summed = jnp.dot(powers, with_ones(txt_kv[1, :, span]), preferred_element_type=jnp.float32)
+        mean_ref[:, here] = summed[:, :head_dim] / summed[:, head_dim:]
+        level_ref[:, here] = highest + jnp.log2(summed[:, head_dim:])
+
+
+def image_kernel(heads, first, time_ref, gate_ref, txt_q_ref, turned_ref, *refs):
+    states, blocks, (img_out_ref, txt_out_ref) = refs[:4], refs[4:-2], refs[-2:]
+    time = time_ref[0]
     rows, width = img_out_ref.shape
     head_dim = width // heads
     text_rows = txt_q_ref.shape[0]
@@ -134,14 +150,11 @@
     image_mask = jnp.where(column < 2 * rows, no_stale, no_fresh)
     text_mask = jnp.broadcast_to(no_stale[:1], (text_rows, columns))
     mask = jnp.concatenate([text_mask, image_mask], axis=0)
-    def store(head, result):
-        span = slice(head * head_dim, (head + 1) * head_dim)
-        txt_out_ref[:, span] = (result[:text_rows] * gate[1:2, span]).astype(jnp.bfloat16)
-        img_out_ref[:, span] = (result[text_rows:] * gate[0:1, span]).astype(jnp.bfloat16)
-
-    waiting = held.shape[0]
     for head in range(heads):
         span = slice(head * head_dim, (head + 1) * head_dim)
+        mean_ref, level_ref = states[:2] if head < first else states[2:]
+        place = head if head < first else head - first
+        here = slice(place * head_dim, (place + 1) * head_dim)
         keys, values = (
             jnp.concatenate(
                 [
@@ -156,22 +169,17 @@
         queries = jnp.concatenate([txt_q_ref[:, span], turned_ref[:, span]], axis=0)
         scores = lax.dot_general(queries, keys, NT, preferred_element_type=jnp.float32)
         scores = scores * scale + mask
-        level = level_ref[:, span]
+        level = level_ref[:, here]
         highest = jnp.maximum(level, jnp.max(scores, axis=-1, keepdims=True))
         weight = jnp.exp2(level - highest)
         powers = jnp.exp2(scores - jnp.concatenate([highest] * (columns // head_dim), axis=1))
         summed = jnp.dot(
             powers.astype(jnp.bfloat16), with_ones(values), preferred_element_type=jnp.float32
         )
-        result = (mean_ref[:, span] * weight + summed[:, :head_dim]) / (weight + summed[:, head_dim:])
-        if head < waiting:
-            held[head] = result
-            if head == waiting - 1:
-                gate_copy.wait()
-                for early in range(waiting):
-                    store(early, held[early])
-        else:
-            store(head, result)
+        result = (mean_ref[:, here] * weight + summed[:, :head_dim]) / (weight + summed[:, head_dim:])
+        gate = gate_ref[time, :, span]
+        txt_out_ref[:, span] = (result[:text_rows] * gate[1:2]).astype(jnp.bfloat16)
+        img_out_ref[:, span] = (result[text_rows:] * gate[0:1]).astype(jnp.bfloat16)
 
 
 def swap(x, even, odd=None):
@@ -181,19 +189,15 @@
     return lax.ppermute(x, "patch", pairs)
 
 
-def gather_columns(block):
+def gather_blocks(block):
     count = lax.axis_size("patch")
-    block = block[None]
     if count == 16:
-        hops = HOPS
-        one = swap(block, *hops[0])
-        three = swap(block, *hops[2])
-        one_two = swap(one, *hops[1])
-        two = swap(block, *hops[1])
-        one_three = swap(one, *hops[2])
-        two_three = swap(two, *hops[2])
-        all_three = swap(one_two, *hops[2])
-        return [block, one, two, three, one_two], [one_three, two_three, all_three]
+        one, two, three = (swap(block, *hop) for hop in HOPS)
+        one_two = swap(one, *HOPS[1])
+        one_three = swap(one, *HOPS[2])
+        two_three = swap(two, *HOPS[2])
+        all_three = swap(one_two, *HOPS[2])
+        return [block, one, two, three], [one_two, one_three, two_three, all_three]
     if count & (count - 1) == 0:
         bit = count // 2
         while bit:
@@ -229,51 +233,68 @@
             pltpu.VMEM(stale_exp.shape, stale_exp.dtype),
             pltpu.SemaphoreType.DMA((3,)),
         ],
+        compiler_params=pltpu.CompilerParams(vmem_limit_bytes=4 << 20),
         name="pack",
     )(order, img_kv, stale_mant, stale_exp)
-    early, late = gather_columns(block)
-    joined = sum(x.shape[0] for x in early)
-    first, *states = pl.pallas_call(
-        functools.partial(text_kernel, heads, len(early)),
+    blocks, late = gather_blocks(block[None])
+    if late:
+        near = join(*blocks)
+        near, order = lax.optimization_barrier((near, order))
+        blocks = [near]
+    share = 2 * heads // 3
+    part = share * (width // heads)
+    gate, txt_q, txt_kv, turned, *state = pl.pallas_call(
+        functools.partial(text_first_kernel, heads, share),
         out_shape=(
-            pltpu.VMEM((joined,) + block.shape, bf16),
+            pltpu.VMEM(gate_table.shape, f32),
             pltpu.VMEM(txt_q.shape, bf16),
+            pltpu.VMEM(txt_kv.shape, bf16),
             pltpu.VMEM((rows, width), bf16),
-            pltpu.VMEM((all_rows, width), f32),
-            pltpu.VMEM((all_rows, width), f32),
+            pltpu.VMEM((all_rows, part), f32),
+            pltpu.VMEM((all_rows, part), f32),
         ),
-        in_specs=[VMEM] + [HBM] * 3 + [VMEM] * len(early),
-        out_specs=[VMEM] * 5,
+        in_specs=[VMEM] + [HBM] * 4,
+        out_specs=[VMEM] * 6,
         scratch_shapes=[
             pltpu.VMEM(img_q.shape, img_q.dtype),
-            pltpu.VMEM(txt_kv.shape, txt_kv.dtype),
-            pltpu.VMEM((heads, all_rows, text_rows), bf16),
-            pltpu.SemaphoreType.DMA((4,)),
-            pltpu.SemaphoreType.DMA((len(early),)),
+            pltpu.VMEM((share, all_rows, text_rows), bf16),
+            pltpu.SemaphoreType.DMA((5,)),
         ],
         compiler_params=pltpu.CompilerParams(vmem_limit_bytes=16 << 20),
-        name="text",
-    )(order, img_q, txt_q, txt_kv, *early)
-    blocks = [first] + late
-    if lax.axis_size("patch") == 16:
-        blocks = list(lax.optimization_barrier(tuple(blocks)))
-        blocks += [swap(x, 1) for x in blocks]
+        name="text_first",
+    )(order, img_q, txt_q, txt_kv, gate_table)
+    if late:
+        near, gate, txt_q, txt_kv, turned, *state = lax.optimization_barrier(
+            (near, gate, txt_q, txt_kv, turned, *state)
+        )
+        blocks = [near, swap(near, 1)]
+    rest = pl.pallas_call(
+        functools.partial(text_second_kernel, heads, share),
+        out_shape=(
+            pltpu.VMEM((all_rows, width - part), f32),
+            pltpu.VMEM((all_rows, width - part), f32),
+        ),
+        in_specs=[VMEM] * 3,
+        out_specs=[VMEM] * 2,
+        compiler_params=pltpu.CompilerParams(vmem_limit_bytes=16 << 20),
+        name="text_second",
+    )(txt_q, txt_kv, turned)
+    states = (gate, txt_q, turned, *state, *rest)
+    if late:
+        far = join(*late)
+        far, *states = lax.optimization_barrier((far, *states))
+        blocks += [far, swap(far, 1)]
     return pl.pallas_call(
-        functools.partial(image_kernel, heads),
+        functools.partial(image_kernel, heads, share),
         out_shape=(
             jax.ShapeDtypeStruct(img_q.shape, bf16),
             jax.ShapeDtypeStruct(txt_q.shape, bf16),
         ),
-        in_specs=[SMEM, HBM] + [VMEM] * (len(states) + len(blocks)),
+        in_specs=[SMEM] + [VMEM] * (len(states) + len(blocks)),
         out_specs=(VMEM, VMEM),
-        scratch_shapes=[
-            pltpu.VMEM(gate_table.shape[1:], f32),
-            pltpu.VMEM((6, all_rows, width // heads), f32),
-            pltpu.SemaphoreType.DMA,
-        ],
         compiler_params=pltpu.CompilerParams(vmem_limit_bytes=32 << 20),
         name="image",
-    )(timestep, gate_table, *states, *blocks)
+    )(timestep, *states, *blocks)
 
 
 def solution(mesh):

time: 24.6 us -> 24 us (0.976)
  starting transfers between devices: 14.8 us -> 14.3 us
    ppermute x11 -> x9, starting transfers between devices: 14.8 us -> 14.3 us  [swap(): return lax.ppermute(x, 'patch', pairs)]
    ppermute x11 -> x9, waiting for transfers between devices: 0.86 us -> 0.71 us  [swap(): return lax.ppermute(x, 'patch', pairs)]
    pallas_call x2 -> x5, Pallas kernels: 5.67 us -> 5.75 us  [the longest x1 2.55 us: on_device(): pl.pallas_call(functools.partial(text_first_kernel, heads, share), out_sh...]
  transfers between devices with their start and end apart: 11 -> 9, of which waited for: 4 -> 1; matrix products, arithmetic and copies ran while one was open for 0% -> 0% of each run, Pallas kernels for 12% -> 14%
where the time goes in v3:
time: 24 us; the launch traced here: 23.8 us
  starting transfers between devices  14.3 us (60%)
  Pallas kernels  6.71 us (28%)
  between operations  2.02 us (8%)
  waiting for transfers between devices  0.71 us (3%)
    ppermute x9, starting transfers between devices, swap(): return lax.ppermute(x, 'patch', pairs)  14.3 us
    pallas_call x1, Pallas kernels, on_device(): pl.pallas_call(functools.partial(text_first_kernel, heads, share), out_sh...  2.55 us
    pallas_call x1, Pallas kernels, on_device(): pl.pallas_call(functools.partial(image_kernel, heads, share), out_shape=(...  2.49 us
    pallas_call x1, Pallas kernels, on_device(): pl.pallas_call(pack_kernel, out_shape=pltpu.VMEM((2 * rows, 2 * width), b...  0.97 us
    ppermute x9, waiting for transfers between devices, swap(): return lax.ppermute(x, 'patch', pairs)  0.71 us
    pallas_call x1, Pallas kernels, on_device(): pl.pallas_call(functools.partial(text_second_kernel, heads, share), out_s...  0.66 us
  transfers between devices with their start and end apart: 9, of which 1 were waited for; matrix products, arithmetic and copies ran while one was open for 0% of the time, Pallas kernels for 14%

profile of v3, /device:TPU:0, one launch (start us, length us, event | category | flops | bytes accessed | tf_op | source)
XLA Modules:
  0.0 23.8 jit_solution(10866932515124898613)
XLA Ops:
  1.3 1.0 %pack.1 = bf16[16,3072]{1,0:T(8,128)(2,1)S(1)} custom-call(s32[1,1]{1,0:T(1,128)} %bitcast.3.order_ref, bf16[2,8,1536]{2,1,0:T(8,128)(2,1)} %kv_hbm.1, bf16[2,8,1536]{2,1,0:T(8,128)(2,1)} %mant_hbm.1, s32[2,8,12]{2,1,0:T(8,128)} %exp_hbm.1), custom_call_target="tpu_custom_call" | custom-call | tf_op jit(solution)/shard_map/pack/pallas_call | solution.py:225
  2.3 3.0 %collective-permute-start = (bf16[1,16,3072]{2,1,0:T(8,128)(2,1)S(1)}, bf16[1,16,3072]{2,1,0:T(8,128)(2,1)S(1)}, u32[]{:S(2)}, u32[]{:S(2)}) collective-permute-start(bf16[1,16,3072]{2,1,0:T(8,128)(2,1)S(1)} %bitcast.4), channel_id=1, source_target_pairs={{0,2},{1,13},{2,0},{3,15},{4,6},{5,9},{6,4},{7,11},{8,10},{9,5},{1... | collective-permute-start | bytes 294920 | tf_op jit(solution)/shard_map/ppermute | solution.py:189
  5.3 2.6 %collective-permute-start.3 = (bf16[1,16,3072]{2,1,0:T(8,128)(2,1)S(1)}, bf16[1,16,3072]{2,1,0:T(8,128)(2,1)S(1)}, u32[]{:S(2)}, u32[]{:S(2)}) collective-permute-start(bf16[1,16,3072]{2,1,0:T(8,128)(2,1)S(1)} %bitcast.5), channel_id=1, source_target_pairs={{0,8},{1,5},{2,10},{3,7},{4,12},{5,1},{6,14},{7,3},{8,0},{9,13},{1... | collective-permute-start | bytes 294920 | tf_op jit(solution)/shard_map/ppermute | solution.py:189
  7.8 0.0 collective-permute-done.refs_1_
  7.9 3.1 %collective-permute-start.1 = (bf16[1,16,3072]{2,1,0:T(8,128)(2,1)S(1)}, bf16[1,16,3072]{2,1,0:T(8,128)(2,1)S(1)}, u32[]{:S(2)}, u32[]{:S(2)}) collective-permute-start(bf16[1,16,3072]{2,1,0:T(8,128)(2,1)S(1)} %collective-permute-done.refs_1_), channel_id=1, source_target_pairs={{0,8},{1,5},{2,10},{3,7},{4,12},{5,1},{6,14},{7,3},{8,0},{9,13},{1... | collective-permute-start | bytes 294920 | tf_op jit(solution)/shard_map/ppermute | solution.py:189
  11.0 1.6 %collective-permute-start.6 = (bf16[1,16,3072]{2,1,0:T(8,128)(2,1)S(1)}, bf16[1,16,3072]{2,1,0:T(8,128)(2,1)S(1)}, u32[]{:S(2)}, u32[]{:S(2)}) collective-permute-start(bf16[1,16,3072]{2,1,0:T(8,128)(2,1)S(1)} %bitcast.6), channel_id=1, source_target_pairs={{0,4},{1,3},{2,6},{3,1},{4,0},{5,7},{6,2},{7,5},{8,12},{9,11},{10,... | collective-permute-start | bytes 294920 | tf_op jit(solution)/shard_map/ppermute | solution.py:189
  12.5 0.4 %collective-permute-start.2 = (bf16[1,16,3072]{2,1,0:T(8,128)(2,1)S(1)}, bf16[1,16,3072]{2,1,0:T(8,128)(2,1)S(1)}, u32[]{:S(2)}, u32[]{:S(2)}) collective-permute-start(bf16[1,16,3072]{2,1,0:T(8,128)(2,1)S(1)} %collective-permute-done.refs_1_), channel_id=1, source_target_pairs={{0,4},{1,3},{2,6},{3,1},{4,0},{5,7},{6,2},{7,5},{8,12},{9,11},{10,... | collective-permute-start | bytes 294920 | tf_op jit(solution)/shard_map/ppermute | solution.py:189
  13.0 0.0 collective-permute-done.3.refs_2_
  13.0 1.6 %collective-permute-start.4 = (bf16[1,16,3072]{2,1,0:T(8,128)(2,1)S(1)}, bf16[1,16,3072]{2,1,0:T(8,128)(2,1)S(1)}, u32[]{:S(2)}, u32[]{:S(2)}) collective-permute-start(bf16[1,16,3072]{2,1,0:T(8,128)(2,1)S(1)} %collective-permute-done.3.refs_2_), channel_id=1, source_target_pairs={{0,4},{1,3},{2,6},{3,1},{4,0},{5,7},{6,2},{7,5},{8,12},{9,11},{10,... | collective-permute-start | bytes 294920 | tf_op jit(solution)/shard_map/ppermute | solution.py:189
  14.6 0.0 collective-permute-done.1.refs_0_
  14.6 1.4 %collective-permute-start.5 = (bf16[1,16,3072]{2,1,0:T(8,128)(2,1)S(1)}, bf16[1,16,3072]{2,1,0:T(8,128)(2,1)S(1)}, u32[]{:S(2)}, u32[]{:S(2)}) collective-permute-start(bf16[1,16,3072]{2,1,0:T(8,128)(2,1)S(1)} %collective-permute-done.1.refs_0_), channel_id=1, source_target_pairs={{0,4},{1,3},{2,6},{3,1},{4,0},{5,7},{6,2},{7,5},{8,12},{9,11},{10,... | collective-permute-start | bytes 294920 | tf_op jit(solution)/shard_map/ppermute | solution.py:189
  16.0 2.5 %text_first.1 = (f32[28,2,1536]{2,1,0:T(2,128)S(1)}, bf16[256,1536]{1,0:T(8,128)(2,1)S(1)}, bf16[2,256,1536]{2,1,0:T(8,128)(2,1)S(1)}, bf16[8,1536]{1,0:T(8,128)...) custom-call(s32[1,1]{1,0:T(1,128)} %bitcast.2.order_ref, bf16[8,1536]{1,0:T(8,128)(2,1)} %q_hbm.1, ...), custom_call_target="tpu_custom_call" | custom-call | tf_op jit(solution)/shard_map/text_first/pallas_call | solution.py:246
  18.5 0.0 collective-permute-done.6.refs_3_
  18.6 0.1 collective-permute-start.7
  18.7 0.7 %text_second.1 = (f32[264,512]{1,0:T(8,128)S(1)}, f32[264,512]{1,0:T(8,128)S(1)}) custom-call(bf16[256,1536]{1,0:T(8,128)(2,1)S(1)} %get-tuple-element.44.txt_q.txt_q_ref, bf16[2,256,1536]{2,1,0:T(8,128)(2,1)S(1)} %get-tuple-element.40.txt_kv, bf16[8,1536]{1,0:T(8,128)(2,1)S(1)} %get-tuple-element.45.turned_ref), custom_call_target="tpu_custom_call" | custom-call | tf_op jit(solution)/shard_map/text_second/pallas_call | solution.py:271
  19.3 0.0 collective-permute-done.2.refs_1_
  19.3 0.0 collective-permute-done.4.refs_2_
  19.4 0.0 collective-permute-done.5.refs_3_
  19.4 0.6 %collective-permute-start.8 = (bf16[4,16,3072]{2,1,0:T(8,128)(2,1)S(1)}, bf16[4,16,3072]{2,1,0:T(8,128)(2,1)S(1)}, u32[]{:S(2)}, u32[]{:S(2)}) collective-permute-start(bf16[4,16,3072]{2,1,0:T(8,128)(2,1)S(1)} %join.2.refs_6_), channel_id=1, source_target_pairs={{0,1},{1,0},{2,3},{3,2},{4,5},{5,4},{6,7},{7,6},{8,9},{9,8},{10,11... | collective-permute-start | bytes 1179656 | tf_op jit(solution)/shard_map/ppermute | solution.py:189
  20.6 0.0 collective-permute-done.7.refs_5_
  20.6 0.7 %collective-permute-done.8.refs_7_ = bf16[4,16,3072]{2,1,0:T(8,128)(2,1)S(1)} collective-permute-done((bf16[4,16,3072]{2,1,0:T(8,128)(2,1)S(1)}, bf16[4,16,3072]{2,1,0:T(8,128)(2,1)S(1)}, u32[]{:S(2)}, u32[]{:S(2)}) %collective-permute-start.8) | collective-permute-done | bytes 393248 | tf_op jit(solution)/shard_map/ppermute | solution.py:189
  21.3 2.5 %image.1 = (bf16[8,1536]{1,0:T(8,128)(2,1)}, bf16[256,1536]{1,0:T(8,128)(2,1)}) custom-call(s32[1]{0:T(128)S(6)} %copy.12.time_ref, f32[28,2,1536]{2,1,0:T(2,128)S(1)} %get-tuple-element.43.gate_ref, bf16[256,1536]{1,0:T(8,128)(2,1)S(1)} %get-tuple-element.44.txt_q.txt_q_ref, bf16[8,1536]{1,0:T(8,128)(2,1)S(1)} %get-tuple-element.45.turned_ref, ...), custom_call_target="tpu_custom_call" | custom-call | tf_op jit(solution)/shard_map/image/pallas_call | solution.py:287
  (2 shorter events, 0.1 us)
Async XLA Ops:
  2.3 5.6 %collective-permute-start = (bf16[1,16,3072]{2,1,0:T(8,128)(2,1)S(1)}, bf16[1,16,3072]{2,1,0:T(8,128)(2,1)S(1)}, u32[]{:S(2)}, u32[]{:S(2)}) collective-permute-start(bf16[1,16,3072]{2,1,0:T(8,128)(2,1)S(1)} %bitcast.4), channel_id=1, source_target_pairs={{0,2},{1,13},{2,0},{3,15},{4,6},{5,9},{6,4},{7,11},{8,10},{9,5},{1... | collective-permute-start | bytes 294920 | tf_op jit(solution)/shard_map/ppermute | solution.py:189
  5.3 7.7 %collective-permute-start.3 = (bf16[1,16,3072]{2,1,0:T(8,128)(2,1)S(1)}, bf16[1,16,3072]{2,1,0:T(8,128)(2,1)S(1)}, u32[]{:S(2)}, u32[]{:S(2)}) collective-permute-start(bf16[1,16,3072]{2,1,0:T(8,128)(2,1)S(1)} %bitcast.5), channel_id=1, source_target_pairs={{0,8},{1,5},{2,10},{3,7},{4,12},{5,1},{6,14},{7,3},{8,0},{9,13},{1... | collective-permute-start | bytes 294920 | tf_op jit(solution)/shard_map/ppermute | solution.py:189
  7.9 6.7 %collective-permute-start.1 = (bf16[1,16,3072]{2,1,0:T(8,128)(2,1)S(1)}, bf16[1,16,3072]{2,1,0:T(8,128)(2,1)S(1)}, u32[]{:S(2)}, u32[]{:S(2)}) collective-permute-start(bf16[1,16,3072]{2,1,0:T(8,128)(2,1)S(1)} %collective-permute-done.refs_1_), channel_id=1, source_target_pairs={{0,8},{1,5},{2,10},{3,7},{4,12},{5,1},{6,14},{7,3},{8,0},{9,13},{1... | collective-permute-start | bytes 294920 | tf_op jit(solution)/shard_map/ppermute | solution.py:189
  11.0 7.6 %collective-permute-start.6 = (bf16[1,16,3072]{2,1,0:T(8,128)(2,1)S(1)}, bf16[1,16,3072]{2,1,0:T(8,128)(2,1)S(1)}, u32[]{:S(2)}, u32[]{:S(2)}) collective-permute-start(bf16[1,16,3072]{2,1,0:T(8,128)(2,1)S(1)} %bitcast.6), channel_id=1, source_target_pairs={{0,4},{1,3},{2,6},{3,1},{4,0},{5,7},{6,2},{7,5},{8,12},{9,11},{10,... | collective-permute-start | bytes 294920 | tf_op jit(solution)/shard_map/ppermute | solution.py:189
  12.5 6.8 %collective-permute-start.2 = (bf16[1,16,3072]{2,1,0:T(8,128)(2,1)S(1)}, bf16[1,16,3072]{2,1,0:T(8,128)(2,1)S(1)}, u32[]{:S(2)}, u32[]{:S(2)}) collective-permute-start(bf16[1,16,3072]{2,1,0:T(8,128)(2,1)S(1)} %collective-permute-done.refs_1_), channel_id=1, source_target_pairs={{0,4},{1,3},{2,6},{3,1},{4,0},{5,7},{6,2},{7,5},{8,12},{9,11},{10,... | collective-permute-start | bytes 294920 | tf_op jit(solution)/shard_map/ppermute | solution.py:189
  13.0 6.3 %collective-permute-start.4 = (bf16[1,16,3072]{2,1,0:T(8,128)(2,1)S(1)}, bf16[1,16,3072]{2,1,0:T(8,128)(2,1)S(1)}, u32[]{:S(2)}, u32[]{:S(2)}) collective-permute-start(bf16[1,16,3072]{2,1,0:T(8,128)(2,1)S(1)} %collective-permute-done.3.refs_2_), channel_id=1, source_target_pairs={{0,4},{1,3},{2,6},{3,1},{4,0},{5,7},{6,2},{7,5},{8,12},{9,11},{10,... | collective-permute-start | bytes 294920 | tf_op jit(solution)/shard_map/ppermute | solution.py:189
  14.6 4.8 %collective-permute-start.5 = (bf16[1,16,3072]{2,1,0:T(8,128)(2,1)S(1)}, bf16[1,16,3072]{2,1,0:T(8,128)(2,1)S(1)}, u32[]{:S(2)}, u32[]{:S(2)}) collective-permute-start(bf16[1,16,3072]{2,1,0:T(8,128)(2,1)S(1)} %collective-permute-done.1.refs_0_), channel_id=1, source_target_pairs={{0,4},{1,3},{2,6},{3,1},{4,0},{5,7},{6,2},{7,5},{8,12},{9,11},{10,... | collective-permute-start | bytes 294920 | tf_op jit(solution)/shard_map/ppermute | solution.py:189
  18.6 2.0 %collective-permute-start.7 = (bf16[4,16,3072]{2,1,0:T(8,128)(2,1)S(1)}, bf16[4,16,3072]{2,1,0:T(8,128)(2,1)S(1)}, u32[]{:S(2)}, u32[]{:S(2)}) collective-permute-start(bf16[4,16,3072]{2,1,0:T(8,128)(2,1)S(1)} %join.3.refs_4_), channel_id=1, source_target_pairs={{0,1},{1,0},{2,3},{3,2},{4,5},{5,4},{6,7},{7,6},{8,9},{9,8},{10,11... | collective-permute-start | bytes 1179656 | tf_op jit(solution)/shard_map/ppermute | solution.py:189
  19.4 1.9 %collective-permute-start.8 = (bf16[4,16,3072]{2,1,0:T(8,128)(2,1)S(1)}, bf16[4,16,3072]{2,1,0:T(8,128)(2,1)S(1)}, u32[]{:S(2)}, u32[]{:S(2)}) collective-permute-start(bf16[4,16,3072]{2,1,0:T(8,128)(2,1)S(1)} %join.2.refs_6_), channel_id=1, source_target_pairs={{0,1},{1,0},{2,3},{3,2},{4,5},{5,4},{6,7},{7,6},{8,9},{9,8},{10,11... | collective-permute-start | bytes 1179656 | tf_op jit(solution)/shard_map/ppermute | solution.py:189

commit v4 on v3

--- a/solution.py
+++ b/solution.py
@@ -60,20 +60,20 @@
             block_ref[:, start : start + head_dim] = both
 
 
-def join_kernel(*refs):
-    for i, block in enumerate(refs[:-1]):
+def join_kernel(count, *refs):
+    for i, block in enumerate(refs[:count]):
         refs[-1][i] = block[0]
 
 
-def join(*blocks):
+def join(blocks, after=()):
     return pl.pallas_call(
-        join_kernel,
+        functools.partial(join_kernel, len(blocks)),
         out_shape=pltpu.VMEM((len(blocks),) + blocks[0].shape[1:], blocks[0].dtype),
-        in_specs=[VMEM] * len(blocks),
+        in_specs=[VMEM] * (len(blocks) + len(after)),
         out_specs=VMEM,
         compiler_params=pltpu.CompilerParams(vmem_limit_bytes=2 << 20),
         name="join",
-    )(*blocks)
+    )(*blocks, *after)
 
 
 def with_ones(values):
@@ -81,7 +81,7 @@
 
 
 def text_first_kernel(heads, share, order_ref, q_hbm, txt_q_hbm, txt_kv_hbm, gate_hbm, *refs):
-    gate_ref, txt_q, txt_kv, turned_ref, mean_ref, level_ref, q, powers_ref, sems = refs
+    gate_ref, txt_q, txt_kv, turned_ref, mean_ref, level_ref, q, powers_ref, sems = refs[-9:]
     q_copy = pltpu.make_async_copy(q_hbm, q, sems.at[0])
     txt_q_copy = pltpu.make_async_copy(txt_q_hbm, txt_q, sems.at[1])
     keys_copy = pltpu.make_async_copy(txt_kv_hbm.at[0], txt_kv.at[0], sems.at[2])
@@ -237,11 +237,8 @@
         name="pack",
     )(order, img_kv, stale_mant, stale_exp)
     blocks, late = gather_blocks(block[None])
-    if late:
-        near = join(*blocks)
-        near, order = lax.optimization_barrier((near, order))
-        blocks = [near]
-    share = 2 * heads // 3
+    waited = blocks if late else []
+    share = heads // 2
     part = share * (width // heads)
     gate, txt_q, txt_kv, turned, *state = pl.pallas_call(
         functools.partial(text_first_kernel, heads, share),
@@ -253,7 +250,7 @@
             pltpu.VMEM((all_rows, part), f32),
             pltpu.VMEM((all_rows, part), f32),
         ),
-        in_specs=[VMEM] + [HBM] * 4,
+        in_specs=[VMEM] + [HBM] * 4 + [VMEM] * len(waited),
         out_specs=[VMEM] * 6,
         scratch_shapes=[
             pltpu.VMEM(img_q.shape, img_q.dtype),
@@ -262,11 +259,9 @@
         ],
         compiler_params=pltpu.CompilerParams(vmem_limit_bytes=16 << 20),
         name="text_first",
-    )(order, img_q, txt_q, txt_kv, gate_table)
+    )(order, img_q, txt_q, txt_kv, gate_table, *waited)
     if late:
-        near, gate, txt_q, txt_kv, turned, *state = lax.optimization_barrier(
-            (near, gate, txt_q, txt_kv, turned, *state)
-        )
+        near = join(blocks, after=(turned,))
         blocks = [near, swap(near, 1)]
     rest = pl.pallas_call(
         functools.partial(text_second_kernel, heads, share),
@@ -281,8 +276,7 @@
     )(txt_q, txt_kv, turned)
     states = (gate, txt_q, turned, *state, *rest)
     if late:
-        far = join(*late)
-        far, *states = lax.optimization_barrier((far, *states))
+        far = join(late, after=())
         blocks += [far, swap(far, 1)]
     return pl.pallas_call(
         functools.partial(image_kernel, heads, share),

time: 24 us -> 23.8 us (level)
  starting transfers between devices: 14.3 us -> 13.9 us
  waiting for transfers between devices: 0.71 us -> 1.04 us
    ppermute x9, starting transfers between devices: 14.3 us -> 13.9 us  [swap(): return lax.ppermute(x, 'patch', pairs)]
    ppermute x9, waiting for transfers between devices: 0.71 us -> 1.04 us  [swap(): return lax.ppermute(x, 'patch', pairs)]
  transfers between devices with their start and end apart: 9 -> 9, of which waited for: 1 -> 2; matrix products, arithmetic and copies ran while one was open for 0% -> 0% of each run, Pallas kernels for 14% -> 14%
where the time goes in v4:
time: 23.8 us; the launch traced here: 23.5 us
  starting transfers between devices  13.9 us (58%)
  Pallas kernels  6.63 us (28%)
  between operations  2.01 us (8%)
  waiting for transfers between devices  1.04 us (4%)
    ppermute x9, starting transfers between devices, swap(): return lax.ppermute(x, 'patch', pairs)  13.9 us
    pallas_call x1, Pallas kernels, on_device(): pl.pallas_call(functools.partial(image_kernel, heads, share), out_shape=(...  2.45 us
    pallas_call x1, Pallas kernels, on_device(): pl.pallas_call(functools.partial(text_first_kernel, heads, share), out_sh...  2.34 us
    ppermute x9, waiting for transfers between devices, swap(): return lax.ppermute(x, 'patch', pairs)  1.04 us
    pallas_call x1, Pallas kernels, on_device(): pl.pallas_call(pack_kernel, out_shape=pltpu.VMEM((2 * rows, 2 * width), b...  0.97 us
    pallas_call x1, Pallas kernels, on_device(): pl.pallas_call(functools.partial(text_second_kernel, heads, share), out_s...  0.82 us
  transfers between devices with their start and end apart: 9, of which 2 were waited for; matrix products, arithmetic and copies ran while one was open for 0% of the time, Pallas kernels for 14%

profile of v4, /device:TPU:0, one launch (start us, length us, event | category | flops | bytes accessed | tf_op | source)
XLA Modules:
  0.0 23.5 jit_solution(14697973679729196564)
XLA Ops:
  1.3 1.0 %pack.1 = bf16[16,3072]{1,0:T(8,128)(2,1)S(1)} custom-call(s32[1,1]{1,0:T(1,128)} %bitcast.2.order_ref, bf16[2,8,1536]{2,1,0:T(8,128)(2,1)} %kv_hbm.1, bf16[2,8,1536]{2,1,0:T(8,128)(2,1)} %mant_hbm.1, s32[2,8,12]{2,1,0:T(8,128)} %exp_hbm.1), custom_call_target="tpu_custom_call" | custom-call | tf_op jit(solution)/shard_map/pack/pallas_call | solution.py:225
  2.3 3.0 %collective-permute-start = (bf16[1,16,3072]{2,1,0:T(8,128)(2,1)S(1)}, bf16[1,16,3072]{2,1,0:T(8,128)(2,1)S(1)}, u32[]{:S(2)}, u32[]{:S(2)}) collective-permute-start(bf16[1,16,3072]{2,1,0:T(8,128)(2,1)S(1)} %bitcast.4), channel_id=1, source_target_pairs={{0,2},{1,13},{2,0},{3,15},{4,6},{5,9},{6,4},{7,11},{8,10},{9,5},{1... | collective-permute-start | bytes 294920 | tf_op jit(solution)/shard_map/ppermute | solution.py:189
  5.3 2.6 %collective-permute-start.1 = (bf16[1,16,3072]{2,1,0:T(8,128)(2,1)S(1)}, bf16[1,16,3072]{2,1,0:T(8,128)(2,1)S(1)}, u32[]{:S(2)}, u32[]{:S(2)}) collective-permute-start(bf16[1,16,3072]{2,1,0:T(8,128)(2,1)S(1)} %bitcast.5), channel_id=1, source_target_pairs={{0,8},{1,5},{2,10},{3,7},{4,12},{5,1},{6,14},{7,3},{8,0},{9,13},{1... | collective-permute-start | bytes 294920 | tf_op jit(solution)/shard_map/ppermute | solution.py:189
  7.8 0.0 collective-permute-done.refs_1_
  7.9 3.1 %collective-permute-start.4 = (bf16[1,16,3072]{2,1,0:T(8,128)(2,1)S(1)}, bf16[1,16,3072]{2,1,0:T(8,128)(2,1)S(1)}, u32[]{:S(2)}, u32[]{:S(2)}) collective-permute-start(bf16[1,16,3072]{2,1,0:T(8,128)(2,1)S(1)} %collective-permute-done.refs_1_), channel_id=1, source_target_pairs={{0,8},{1,5},{2,10},{3,7},{4,12},{5,1},{6,14},{7,3},{8,0},{9,13},{1... | collective-permute-start | bytes 294920 | tf_op jit(solution)/shard_map/ppermute | solution.py:189
  11.0 1.6 %collective-permute-start.2 = (bf16[1,16,3072]{2,1,0:T(8,128)(2,1)S(1)}, bf16[1,16,3072]{2,1,0:T(8,128)(2,1)S(1)}, u32[]{:S(2)}, u32[]{:S(2)}) collective-permute-start(bf16[1,16,3072]{2,1,0:T(8,128)(2,1)S(1)} %bitcast.6), channel_id=1, source_target_pairs={{0,4},{1,3},{2,6},{3,1},{4,0},{5,7},{6,2},{7,5},{8,12},{9,11},{10,... | collective-permute-start | bytes 294920 | tf_op jit(solution)/shard_map/ppermute | solution.py:189
  12.5 0.4 %collective-permute-start.5 = (bf16[1,16,3072]{2,1,0:T(8,128)(2,1)S(1)}, bf16[1,16,3072]{2,1,0:T(8,128)(2,1)S(1)}, u32[]{:S(2)}, u32[]{:S(2)}) collective-permute-start(bf16[1,16,3072]{2,1,0:T(8,128)(2,1)S(1)} %collective-permute-done.refs_1_), channel_id=1, source_target_pairs={{0,4},{1,3},{2,6},{3,1},{4,0},{5,7},{6,2},{7,5},{8,12},{9,11},{10,... | collective-permute-start | bytes 294920 | tf_op jit(solution)/shard_map/ppermute | solution.py:189
  13.0 0.0 collective-permute-done.1.refs_2_
  13.0 1.6 %collective-permute-start.6 = (bf16[1,16,3072]{2,1,0:T(8,128)(2,1)S(1)}, bf16[1,16,3072]{2,1,0:T(8,128)(2,1)S(1)}, u32[]{:S(2)}, u32[]{:S(2)}) collective-permute-start(bf16[1,16,3072]{2,1,0:T(8,128)(2,1)S(1)} %collective-permute-done.1.refs_2_), channel_id=1, source_target_pairs={{0,4},{1,3},{2,6},{3,1},{4,0},{5,7},{6,2},{7,5},{8,12},{9,11},{10,... | collective-permute-start | bytes 294920 | tf_op jit(solution)/shard_map/ppermute | solution.py:189
  14.6 0.0 collective-permute-done.4.refs_0_
  14.6 1.4 %collective-permute-start.7 = (bf16[1,16,3072]{2,1,0:T(8,128)(2,1)S(1)}, bf16[1,16,3072]{2,1,0:T(8,128)(2,1)S(1)}, u32[]{:S(2)}, u32[]{:S(2)}) collective-permute-start(bf16[1,16,3072]{2,1,0:T(8,128)(2,1)S(1)} %collective-permute-done.4.refs_0_), channel_id=1, source_target_pairs={{0,4},{1,3},{2,6},{3,1},{4,0},{5,7},{6,2},{7,5},{8,12},{9,11},{10,... | collective-permute-start | bytes 294920 | tf_op jit(solution)/shard_map/ppermute | solution.py:189
  16.0 0.0 collective-permute-done.2.refs_3_
  16.0 2.3 %text_first.1 = (f32[28,2,1536]{2,1,0:T(2,128)S(1)}, bf16[256,1536]{1,0:T(8,128)(2,1)S(1)}, bf16[2,256,1536]{2,1,0:T(8,128)(2,1)S(1)}, bf16[8,1536]{1,0:T(8,128)...) custom-call(s32[1,1]{1,0:T(1,128)} %bitcast.3.order_ref, bf16[8,1536]{1,0:T(8,128)(2,1)} %q_hbm.1, ...), custom_call_target="tpu_custom_call" | custom-call | tf_op jit(solution)/shard_map/text_first/pallas_call | solution.py:243
  18.4 0.1 collective-permute-start.3
  18.5 0.0 collective-permute-done.5.refs_1_
  18.5 0.0 collective-permute-done.6.refs_2_
  18.5 0.8 %collective-permute-done.7.refs_3_ = bf16[1,16,3072]{2,1,0:T(8,128)(2,1)S(1)} collective-permute-done((bf16[1,16,3072]{2,1,0:T(8,128)(2,1)S(1)}, bf16[1,16,3072]{2,1,0:T(8,128)(2,1)S(1)}, u32[]{:S(2)}, u32[]{:S(2)}) %collective-permute-start.7) | collective-permute-done | bytes 98336 | tf_op jit(solution)/shard_map/ppermute | solution.py:189
  19.3 0.1 collective-permute-start.8
  20.0 0.8 %text_second.1 = (f32[264,768]{1,0:T(8,128)S(1)}, f32[264,768]{1,0:T(8,128)S(1)}) custom-call(bf16[256,1536]{1,0:T(8,128)(2,1)S(1)} %get-tuple-element.11.txt_q.txt_q_ref, bf16[2,256,1536]{2,1,0:T(8,128)(2,1)S(1)} %get-tuple-element.15.txt_kv, bf16[8,1536]{1,0:T(8,128)(2,1)S(1)} %get-tuple-element.12.turned_ref.refs_4_), custom_call_target="tpu_custom_call" | custom-call | tf_op jit(solution)/shard_map/text_second/pallas_call | solution.py:266
  20.9 0.0 collective-permute-done.3.refs_5_
  20.9 0.2 collective-permute-done.8.refs_7_
  21.1 2.5 %image.1 = (bf16[8,1536]{1,0:T(8,128)(2,1)}, bf16[256,1536]{1,0:T(8,128)(2,1)}) custom-call(s32[1]{0:T(128)S(6)} %copy.12.time_ref, f32[28,2,1536]{2,1,0:T(2,128)S(1)} %get-tuple-element.10.gate_ref, bf16[256,1536]{1,0:T(8,128)(2,1)S(1)} %get-tuple-element.11.txt_q.txt_q_ref, bf16[8,1536]{1,0:T(8,128)(2,1)S(1)} %get-tuple-element.12.turned_ref.refs_4_, ...), custom_call_target="tpu_custom_call" | custom-call | tf_op jit(solution)/shard_map/image/pallas_call | solution.py:281
  (2 shorter events, 0.1 us)
Async XLA Ops:
  2.3 5.6 %collective-permute-start = (bf16[1,16,3072]{2,1,0:T(8,128)(2,1)S(1)}, bf16[1,16,3072]{2,1,0:T(8,128)(2,1)S(1)}, u32[]{:S(2)}, u32[]{:S(2)}) collective-permute-start(bf16[1,16,3072]{2,1,0:T(8,128)(2,1)S(1)} %bitcast.4), channel_id=1, source_target_pairs={{0,2},{1,13},{2,0},{3,15},{4,6},{5,9},{6,4},{7,11},{8,10},{9,5},{1... | collective-permute-start | bytes 294920 | tf_op jit(solution)/shard_map/ppermute | solution.py:189
  5.3 7.7 %collective-permute-start.1 = (bf16[1,16,3072]{2,1,0:T(8,128)(2,1)S(1)}, bf16[1,16,3072]{2,1,0:T(8,128)(2,1)S(1)}, u32[]{:S(2)}, u32[]{:S(2)}) collective-permute-start(bf16[1,16,3072]{2,1,0:T(8,128)(2,1)S(1)} %bitcast.5), channel_id=1, source_target_pairs={{0,8},{1,5},{2,10},{3,7},{4,12},{5,1},{6,14},{7,3},{8,0},{9,13},{1... | collective-permute-start | bytes 294920 | tf_op jit(solution)/shard_map/ppermute | solution.py:189
  7.9 6.7 %collective-permute-start.4 = (bf16[1,16,3072]{2,1,0:T(8,128)(2,1)S(1)}, bf16[1,16,3072]{2,1,0:T(8,128)(2,1)S(1)}, u32[]{:S(2)}, u32[]{:S(2)}) collective-permute-start(bf16[1,16,3072]{2,1,0:T(8,128)(2,1)S(1)} %collective-permute-done.refs_1_), channel_id=1, source_target_pairs={{0,8},{1,5},{2,10},{3,7},{4,12},{5,1},{6,14},{7,3},{8,0},{9,13},{1... | collective-permute-start | bytes 294920 | tf_op jit(solution)/shard_map/ppermute | solution.py:189
  11.0 5.0 %collective-permute-start.2 = (bf16[1,16,3072]{2,1,0:T(8,128)(2,1)S(1)}, bf16[1,16,3072]{2,1,0:T(8,128)(2,1)S(1)}, u32[]{:S(2)}, u32[]{:S(2)}) collective-permute-start(bf16[1,16,3072]{2,1,0:T(8,128)(2,1)S(1)} %bitcast.6), channel_id=1, source_target_pairs={{0,4},{1,3},{2,6},{3,1},{4,0},{5,7},{6,2},{7,5},{8,12},{9,11},{10,... | collective-permute-start | bytes 294920 | tf_op jit(solution)/shard_map/ppermute | solution.py:189
  12.5 5.9 %collective-permute-start.5 = (bf16[1,16,3072]{2,1,0:T(8,128)(2,1)S(1)}, bf16[1,16,3072]{2,1,0:T(8,128)(2,1)S(1)}, u32[]{:S(2)}, u32[]{:S(2)}) collective-permute-start(bf16[1,16,3072]{2,1,0:T(8,128)(2,1)S(1)} %collective-permute-done.refs_1_), channel_id=1, source_target_pairs={{0,4},{1,3},{2,6},{3,1},{4,0},{5,7},{6,2},{7,5},{8,12},{9,11},{10,... | collective-permute-start | bytes 294920 | tf_op jit(solution)/shard_map/ppermute | solution.py:189
  13.0 5.5 %collective-permute-start.6 = (bf16[1,16,3072]{2,1,0:T(8,128)(2,1)S(1)}, bf16[1,16,3072]{2,1,0:T(8,128)(2,1)S(1)}, u32[]{:S(2)}, u32[]{:S(2)}) collective-permute-start(bf16[1,16,3072]{2,1,0:T(8,128)(2,1)S(1)} %collective-permute-done.1.refs_2_), channel_id=1, source_target_pairs={{0,4},{1,3},{2,6},{3,1},{4,0},{5,7},{6,2},{7,5},{8,12},{9,11},{10,... | collective-permute-start | bytes 294920 | tf_op jit(solution)/shard_map/ppermute | solution.py:189
  14.6 4.7 %collective-permute-start.7 = (bf16[1,16,3072]{2,1,0:T(8,128)(2,1)S(1)}, bf16[1,16,3072]{2,1,0:T(8,128)(2,1)S(1)}, u32[]{:S(2)}, u32[]{:S(2)}) collective-permute-start(bf16[1,16,3072]{2,1,0:T(8,128)(2,1)S(1)} %collective-permute-done.4.refs_0_), channel_id=1, source_target_pairs={{0,4},{1,3},{2,6},{3,1},{4,0},{5,7},{6,2},{7,5},{8,12},{9,11},{10,... | collective-permute-start | bytes 294920 | tf_op jit(solution)/shard_map/ppermute | solution.py:189
  18.4 2.5 %collective-permute-start.3 = (bf16[4,16,3072]{2,1,0:T(8,128)(2,1)S(1)}, bf16[4,16,3072]{2,1,0:T(8,128)(2,1)S(1)}, u32[]{:S(2)}, u32[]{:S(2)}) collective-permute-start(bf16[4,16,3072]{2,1,0:T(8,128)(2,1)S(1)} %join.2.refs_4_), channel_id=1, source_target_pairs={{0,1},{1,0},{2,3},{3,2},{4,5},{5,4},{6,7},{7,6},{8,9},{9,8},{10,11... | collective-permute-start | bytes 1179656 | tf_op jit(solution)/shard_map/ppermute | solution.py:189
  19.3 1.8 %collective-permute-start.8 = (bf16[4,16,3072]{2,1,0:T(8,128)(2,1)S(1)}, bf16[4,16,3072]{2,1,0:T(8,128)(2,1)S(1)}, u32[]{:S(2)}, u32[]{:S(2)}) collective-permute-start(bf16[4,16,3072]{2,1,0:T(8,128)(2,1)S(1)} %join.3.refs_6_), channel_id=1, source_target_pairs={{0,1},{1,0},{2,3},{3,2},{4,5},{5,4},{6,7},{7,6},{8,9},{9,8},{10,11... | collective-permute-start | bytes 1179656 | tf_op jit(solution)/shard_map/ppermute | solution.py:189

commit v5 on v4

--- a/solution.py
+++ b/solution.py
@@ -148,8 +148,7 @@
     no_stale = jnp.where(fresh, 0.0, HIDDEN)
     no_fresh = jnp.where(fresh, HIDDEN, 0.0)
     image_mask = jnp.where(column < 2 * rows, no_stale, no_fresh)
-    text_mask = jnp.broadcast_to(no_stale[:1], (text_rows, columns))
-    mask = jnp.concatenate([text_mask, image_mask], axis=0)
+    text_mask = no_stale[:1]
     for head in range(heads):
         span = slice(head * head_dim, (head + 1) * head_dim)
         mean_ref, level_ref = states[:2] if head < first else states[2:]
@@ -168,7 +167,9 @@
         )
         queries = jnp.concatenate([txt_q_ref[:, span], turned_ref[:, span]], axis=0)
         scores = lax.dot_general(queries, keys, NT, preferred_element_type=jnp.float32)
-        scores = scores * scale + mask
+        scores = jnp.concatenate(
+            [scores[:text_rows] * scale + text_mask, scores[text_rows:] * scale + image_mask], axis=0
+        )
         level = level_ref[:, here]
         highest = jnp.maximum(level, jnp.max(scores, axis=-1, keepdims=True))
         weight = jnp.exp2(level - highest)
@@ -237,7 +238,10 @@
         name="pack",
     )(order, img_kv, stale_mant, stale_exp)
     blocks, late = gather_blocks(block[None])
-    waited = blocks if late else []
+    waited = []
+    if late:
+        near = join(blocks)
+        waited = [near]
     share = heads // 2
     part = share * (width // heads)
     gate, txt_q, txt_kv, turned, *state = pl.pallas_call(
@@ -261,7 +265,6 @@
         name="text_first",
     )(order, img_q, txt_q, txt_kv, gate_table, *waited)
     if late:
-        near = join(blocks, after=(turned,))
         blocks = [near, swap(near, 1)]
     rest = pl.pallas_call(
         functools.partial(text_second_kernel, heads, share),
@@ -276,7 +279,7 @@
     )(txt_q, txt_kv, turned)
     states = (gate, txt_q, turned, *state, *rest)
     if late:
-        far = join(late, after=())
+        far = join(late, after=(turned,))
         blocks += [far, swap(far, 1)]
     return pl.pallas_call(
         functools.partial(image_kernel, heads, share),

time: 23.8 us -> 23.8 us (level)
  no operation moved by 1% of the time
where the time goes in v5:
time: 23.8 us; the launch traced here: 23.6 us
  starting transfers between devices  13.9 us (58%)
  Pallas kernels  6.65 us (28%)
  between operations  2 us (8%)
  waiting for transfers between devices  1.04 us (4%)
    ppermute x9, starting transfers between devices, swap(): return lax.ppermute(x, 'patch', pairs)  13.9 us
    pallas_call x1, Pallas kernels, on_device(): pl.pallas_call(functools.partial(image_kernel, heads, share), out_shape=(...  2.46 us
    pallas_call x1, Pallas kernels, on_device(): pl.pallas_call(functools.partial(text_first_kernel, heads, share), out_sh...  2.35 us
    ppermute x9, waiting for transfers between devices, swap(): return lax.ppermute(x, 'patch', pairs)  1.04 us
    pallas_call x1, Pallas kernels, on_device(): pl.pallas_call(pack_kernel, out_shape=pltpu.VMEM((2 * rows, 2 * width), b...  0.97 us
    pallas_call x1, Pallas kernels, on_device(): pl.pallas_call(functools.partial(text_second_kernel, heads, share), out_s...  0.82 us
  transfers between devices with their start and end apart: 9, of which 2 were waited for; matrix products, arithmetic and copies ran while one was open for 0% of the time, Pallas kernels for 14%

profile of v5, /device:TPU:0, one launch (start us, length us, event | category | flops | bytes accessed | tf_op | source)
XLA Modules:
  0.0 23.6 jit_solution(17079786969138651036)
XLA Ops:
  1.3 1.0 %pack.1 = bf16[16,3072]{1,0:T(8,128)(2,1)S(1)} custom-call(s32[1,1]{1,0:T(1,128)} %bitcast.2.order_ref, bf16[2,8,1536]{2,1,0:T(8,128)(2,1)} %kv_hbm.1, bf16[2,8,1536]{2,1,0:T(8,128)(2,1)} %mant_hbm.1, s32[2,8,12]{2,1,0:T(8,128)} %exp_hbm.1), custom_call_target="tpu_custom_call" | custom-call | tf_op jit(solution)/shard_map/pack/pallas_call | solution.py:226
  2.3 3.0 %collective-permute-start = (bf16[1,16,3072]{2,1,0:T(8,128)(2,1)S(1)}, bf16[1,16,3072]{2,1,0:T(8,128)(2,1)S(1)}, u32[]{:S(2)}, u32[]{:S(2)}) collective-permute-start(bf16[1,16,3072]{2,1,0:T(8,128)(2,1)S(1)} %bitcast.4), channel_id=1, source_target_pairs={{0,2},{1,13},{2,0},{3,15},{4,6},{5,9},{6,4},{7,11},{8,10},{9,5},{1... | collective-permute-start | bytes 294920 | tf_op jit(solution)/shard_map/ppermute | solution.py:190
  5.3 2.6 %collective-permute-start.1 = (bf16[1,16,3072]{2,1,0:T(8,128)(2,1)S(1)}, bf16[1,16,3072]{2,1,0:T(8,128)(2,1)S(1)}, u32[]{:S(2)}, u32[]{:S(2)}) collective-permute-start(bf16[1,16,3072]{2,1,0:T(8,128)(2,1)S(1)} %bitcast.5), channel_id=1, source_target_pairs={{0,8},{1,5},{2,10},{3,7},{4,12},{5,1},{6,14},{7,3},{8,0},{9,13},{1... | collective-permute-start | bytes 294920 | tf_op jit(solution)/shard_map/ppermute | solution.py:190
  7.8 0.0 collective-permute-done.refs_1_
  7.9 3.1 %collective-permute-start.4 = (bf16[1,16,3072]{2,1,0:T(8,128)(2,1)S(1)}, bf16[1,16,3072]{2,1,0:T(8,128)(2,1)S(1)}, u32[]{:S(2)}, u32[]{:S(2)}) collective-permute-start(bf16[1,16,3072]{2,1,0:T(8,128)(2,1)S(1)} %collective-permute-done.refs_1_), channel_id=1, source_target_pairs={{0,8},{1,5},{2,10},{3,7},{4,12},{5,1},{6,14},{7,3},{8,0},{9,13},{1... | collective-permute-start | bytes 294920 | tf_op jit(solution)/shard_map/ppermute | solution.py:190
  11.0 1.6 %collective-permute-start.2 = (bf16[1,16,3072]{2,1,0:T(8,128)(2,1)S(1)}, bf16[1,16,3072]{2,1,0:T(8,128)(2,1)S(1)}, u32[]{:S(2)}, u32[]{:S(2)}) collective-permute-start(bf16[1,16,3072]{2,1,0:T(8,128)(2,1)S(1)} %bitcast.6), channel_id=1, source_target_pairs={{0,4},{1,3},{2,6},{3,1},{4,0},{5,7},{6,2},{7,5},{8,12},{9,11},{10,... | collective-permute-start | bytes 294920 | tf_op jit(solution)/shard_map/ppermute | solution.py:190
  12.5 0.4 %collective-permute-start.5 = (bf16[1,16,3072]{2,1,0:T(8,128)(2,1)S(1)}, bf16[1,16,3072]{2,1,0:T(8,128)(2,1)S(1)}, u32[]{:S(2)}, u32[]{:S(2)}) collective-permute-start(bf16[1,16,3072]{2,1,0:T(8,128)(2,1)S(1)} %collective-permute-done.refs_1_), channel_id=1, source_target_pairs={{0,4},{1,3},{2,6},{3,1},{4,0},{5,7},{6,2},{7,5},{8,12},{9,11},{10,... | collective-permute-start | bytes 294920 | tf_op jit(solution)/shard_map/ppermute | solution.py:190
  13.0 0.0 collective-permute-done.1.refs_2_
  13.0 1.6 %collective-permute-start.6 = (bf16[1,16,3072]{2,1,0:T(8,128)(2,1)S(1)}, bf16[1,16,3072]{2,1,0:T(8,128)(2,1)S(1)}, u32[]{:S(2)}, u32[]{:S(2)}) collective-permute-start(bf16[1,16,3072]{2,1,0:T(8,128)(2,1)S(1)} %collective-permute-done.1.refs_2_), channel_id=1, source_target_pairs={{0,4},{1,3},{2,6},{3,1},{4,0},{5,7},{6,2},{7,5},{8,12},{9,11},{10,... | collective-permute-start | bytes 294920 | tf_op jit(solution)/shard_map/ppermute | solution.py:190
  14.6 0.0 collective-permute-done.4.refs_0_
  14.6 1.4 %collective-permute-start.7 = (bf16[1,16,3072]{2,1,0:T(8,128)(2,1)S(1)}, bf16[1,16,3072]{2,1,0:T(8,128)(2,1)S(1)}, u32[]{:S(2)}, u32[]{:S(2)}) collective-permute-start(bf16[1,16,3072]{2,1,0:T(8,128)(2,1)S(1)} %collective-permute-done.4.refs_0_), channel_id=1, source_target_pairs={{0,4},{1,3},{2,6},{3,1},{4,0},{5,7},{6,2},{7,5},{8,12},{9,11},{10,... | collective-permute-start | bytes 294920 | tf_op jit(solution)/shard_map/ppermute | solution.py:190
  16.0 0.0 collective-permute-done.2.refs_3_
  16.0 0.1 collective-permute-start.3
  16.1 2.4 %text_first.1 = (f32[28,2,1536]{2,1,0:T(2,128)S(1)}, bf16[256,1536]{1,0:T(8,128)(2,1)S(1)}, bf16[2,256,1536]{2,1,0:T(8,128)(2,1)S(1)}, bf16[8,1536]{1,0:T(8,128)...) custom-call(s32[1,1]{1,0:T(1,128)} %bitcast.3.order_ref, bf16[8,1536]{1,0:T(8,128)(2,1)} %q_hbm.1, ...), custom_call_target="tpu_custom_call" | custom-call | tf_op jit(solution)/shard_map/text_first/pallas_call | solution.py:247
  18.5 0.0 collective-permute-done.5.refs_1_
  18.5 0.0 collective-permute-done.6.refs_2_
  18.5 0.8 %collective-permute-done.7.refs_3_ = bf16[1,16,3072]{2,1,0:T(8,128)(2,1)S(1)} collective-permute-done((bf16[1,16,3072]{2,1,0:T(8,128)(2,1)S(1)}, bf16[1,16,3072]{2,1,0:T(8,128)(2,1)S(1)}, u32[]{:S(2)}, u32[]{:S(2)}) %collective-permute-start.7) | collective-permute-done | bytes 98336 | tf_op jit(solution)/shard_map/ppermute | solution.py:190
  19.3 0.1 collective-permute-start.8
  20.0 0.8 %text_second.1 = (f32[264,768]{1,0:T(8,128)S(1)}, f32[264,768]{1,0:T(8,128)S(1)}) custom-call(bf16[256,1536]{1,0:T(8,128)(2,1)S(1)} %get-tuple-element.11.txt_q.txt_q_ref, bf16[2,256,1536]{2,1,0:T(8,128)(2,1)S(1)} %get-tuple-element.15.txt_kv, bf16[8,1536]{1,0:T(8,128)(2,1)S(1)} %get-tuple-element.12.turned_ref.refs_4_), custom_call_target="tpu_custom_call" | custom-call | tf_op jit(solution)/shard_map/text_second/pallas_call | solution.py:269
  20.9 0.0 collective-permute-done.3.refs_5_
  20.9 0.2 collective-permute-done.8.refs_7_
  21.1 2.5 %image.1 = (bf16[8,1536]{1,0:T(8,128)(2,1)}, bf16[256,1536]{1,0:T(8,128)(2,1)}) custom-call(s32[1]{0:T(128)S(6)} %copy.12.time_ref, f32[28,2,1536]{2,1,0:T(2,128)S(1)} %get-tuple-element.10.gate_ref, bf16[256,1536]{1,0:T(8,128)(2,1)S(1)} %get-tuple-element.11.txt_q.txt_q_ref, bf16[8,1536]{1,0:T(8,128)(2,1)S(1)} %get-tuple-element.12.turned_ref.refs_4_, ...), custom_call_target="tpu_custom_call" | custom-call | tf_op jit(solution)/shard_map/image/pallas_call | solution.py:284
  (2 shorter events, 0.1 us)
Async XLA Ops:
  2.3 5.6 %collective-permute-start = (bf16[1,16,3072]{2,1,0:T(8,128)(2,1)S(1)}, bf16[1,16,3072]{2,1,0:T(8,128)(2,1)S(1)}, u32[]{:S(2)}, u32[]{:S(2)}) collective-permute-start(bf16[1,16,3072]{2,1,0:T(8,128)(2,1)S(1)} %bitcast.4), channel_id=1, source_target_pairs={{0,2},{1,13},{2,0},{3,15},{4,6},{5,9},{6,4},{7,11},{8,10},{9,5},{1... | collective-permute-start | bytes 294920 | tf_op jit(solution)/shard_map/ppermute | solution.py:190
  5.3 7.7 %collective-permute-start.1 = (bf16[1,16,3072]{2,1,0:T(8,128)(2,1)S(1)}, bf16[1,16,3072]{2,1,0:T(8,128)(2,1)S(1)}, u32[]{:S(2)}, u32[]{:S(2)}) collective-permute-start(bf16[1,16,3072]{2,1,0:T(8,128)(2,1)S(1)} %bitcast.5), channel_id=1, source_target_pairs={{0,8},{1,5},{2,10},{3,7},{4,12},{5,1},{6,14},{7,3},{8,0},{9,13},{1... | collective-permute-start | bytes 294920 | tf_op jit(solution)/shard_map/ppermute | solution.py:190
  7.9 6.7 %collective-permute-start.4 = (bf16[1,16,3072]{2,1,0:T(8,128)(2,1)S(1)}, bf16[1,16,3072]{2,1,0:T(8,128)(2,1)S(1)}, u32[]{:S(2)}, u32[]{:S(2)}) collective-permute-start(bf16[1,16,3072]{2,1,0:T(8,128)(2,1)S(1)} %collective-permute-done.refs_1_), channel_id=1, source_target_pairs={{0,8},{1,5},{2,10},{3,7},{4,12},{5,1},{6,14},{7,3},{8,0},{9,13},{1... | collective-permute-start | bytes 294920 | tf_op jit(solution)/shard_map/ppermute | solution.py:190
  11.0 5.0 %collective-permute-start.2 = (bf16[1,16,3072]{2,1,0:T(8,128)(2,1)S(1)}, bf16[1,16,3072]{2,1,0:T(8,128)(2,1)S(1)}, u32[]{:S(2)}, u32[]{:S(2)}) collective-permute-start(bf16[1,16,3072]{2,1,0:T(8,128)(2,1)S(1)} %bitcast.6), channel_id=1, source_target_pairs={{0,4},{1,3},{2,6},{3,1},{4,0},{5,7},{6,2},{7,5},{8,12},{9,11},{10,... | collective-permute-start | bytes 294920 | tf_op jit(solution)/shard_map/ppermute | solution.py:190
  12.5 5.9 %collective-permute-start.5 = (bf16[1,16,3072]{2,1,0:T(8,128)(2,1)S(1)}, bf16[1,16,3072]{2,1,0:T(8,128)(2,1)S(1)}, u32[]{:S(2)}, u32[]{:S(2)}) collective-permute-start(bf16[1,16,3072]{2,1,0:T(8,128)(2,1)S(1)} %collective-permute-done.refs_1_), channel_id=1, source_target_pairs={{0,4},{1,3},{2,6},{3,1},{4,0},{5,7},{6,2},{7,5},{8,12},{9,11},{10,... | collective-permute-start | bytes 294920 | tf_op jit(solution)/shard_map/ppermute | solution.py:190
  13.0 5.5 %collective-permute-start.6 = (bf16[1,16,3072]{2,1,0:T(8,128)(2,1)S(1)}, bf16[1,16,3072]{2,1,0:T(8,128)(2,1)S(1)}, u32[]{:S(2)}, u32[]{:S(2)}) collective-permute-start(bf16[1,16,3072]{2,1,0:T(8,128)(2,1)S(1)} %collective-permute-done.1.refs_2_), channel_id=1, source_target_pairs={{0,4},{1,3},{2,6},{3,1},{4,0},{5,7},{6,2},{7,5},{8,12},{9,11},{10,... | collective-permute-start | bytes 294920 | tf_op jit(solution)/shard_map/ppermute | solution.py:190
  14.6 4.7 %collective-permute-start.7 = (bf16[1,16,3072]{2,1,0:T(8,128)(2,1)S(1)}, bf16[1,16,3072]{2,1,0:T(8,128)(2,1)S(1)}, u32[]{:S(2)}, u32[]{:S(2)}) collective-permute-start(bf16[1,16,3072]{2,1,0:T(8,128)(2,1)S(1)} %collective-permute-done.4.refs_0_), channel_id=1, source_target_pairs={{0,4},{1,3},{2,6},{3,1},{4,0},{5,7},{6,2},{7,5},{8,12},{9,11},{10,... | collective-permute-start | bytes 294920 | tf_op jit(solution)/shard_map/ppermute | solution.py:190
  16.0 4.8 %collective-permute-start.3 = (bf16[4,16,3072]{2,1,0:T(8,128)(2,1)S(1)}, bf16[4,16,3072]{2,1,0:T(8,128)(2,1)S(1)}, u32[]{:S(2)}, u32[]{:S(2)}) collective-permute-start(bf16[4,16,3072]{2,1,0:T(8,128)(2,1)S(1)} %join.2.refs_0_.refs_4_), channel_id=1, source_target_pairs={{0,1},{1,0},{2,3},{3,2},{4,5},{5,4},{6,7},{7,6},{8,9},{9,8},{10,11... | collective-permute-start | bytes 1179656 | tf_op jit(solution)/shard_map/ppermute | solution.py:190
  19.3 1.8 %collective-permute-start.8 = (bf16[4,16,3072]{2,1,0:T(8,128)(2,1)S(1)}, bf16[4,16,3072]{2,1,0:T(8,128)(2,1)S(1)}, u32[]{:S(2)}, u32[]{:S(2)}) collective-permute-start(bf16[4,16,3072]{2,1,0:T(8,128)(2,1)S(1)} %join.3.refs_6_), channel_id=1, source_target_pairs={{0,1},{1,0},{2,3},{3,2},{4,5},{5,4},{6,7},{7,6},{8,9},{9,8},{10,11... | collective-permute-start | bytes 1179656 | tf_op jit(solution)/shard_map/ppermute | solution.py:190
